TPU v7x, 256 devices: a whole 4x4x8 slice. The times are simulated.
256 devices in a mesh: row: 16 (over y, z_hi), col: 16 (over x, z_lo, core).
Axes of the slice: x: 4, y: 4, z: 8 (z_hi: 4, z_lo: 2; z = z_hi * 2 + z_lo), core: 2. Of those that a mesh axis runs over, the one named last changes fastest.
Arguments:
- inputs: bfloat16 [131072, 256], P(('row', 'col')), may hold values from -6 to 6
- aggregated: bfloat16 [131072, 256], P(('row', 'col')), may hold values from -6 to 6
- grad_out: bfloat16 [131072, 256], P(('row', 'col')), may hold values from -6 to 6
- preact: bfloat16 [131072, 256], P(('row', 'col')), may hold values from -6 to 6
- inv_degree: bfloat16 [131072], P(('row', 'col')), may hold values from 0.099609375 to 1
- w_self: bfloat16 [256, 256], replicated, may hold values from -0.375 to 0.375
- w_neigh: bfloat16 [256, 256], replicated, may hold values from -0.375 to 0.375
- blocks: bfloat16 [86016, 128, 128], P(('row', 'col')), may hold values from 0 to 0.079589844
- block_rows: int32 [86016], P(('row', 'col')), may hold values from 0 to 63
- block_cols: int32 [86016], P(('row', 'col')), may hold values from 0 to 63
- block_count: int32 [16, 16], P('row', 'col'), may hold values from 42 to 336, as said below
Outputs:
- grad_inputs: bfloat16 [131072, 256], P(('row', 'col'))
- grad_self: float32 [256, 256], replicated
- grad_neigh: float32 [256, 256], replicated
- grad_bias: float32 [256], replicated
Inputs may be any that keep to these rules, and one draw needn't show every extreme that they name: `block_count`: some grid cell has exactly 336 live slots.
All inputs are finite; a program needn't handle non-finite values.
Results may differ from a plain program's by a relative error of at most 0.015.
Values may be sent and summed in bfloat16 or wider, within the bound.
A program may use at most 128 MiB of HBM per device.

v0:
```python
import jax
import jax.numpy as jnp
from jax import lax
from jax.sharding import PartitionSpec as P


def local(
    inputs,
    aggregated,
    grad_out,
    preact,
    inv_degree,
    w_self,
    w_neigh,
    blocks,
    block_rows,
    block_cols,
    block_count,
):
    masked = jnp.where(preact > 0, grad_out, jnp.zeros_like(grad_out))
    projected = jnp.dot(masked, w_neigh.T, preferred_element_type=jnp.float32)
    local_grads = (projected * inv_degree.astype(jnp.float32)[:, None]).astype(jnp.bfloat16)
    strip_grads = lax.all_gather(local_grads, "col", axis=0, tiled=True)
    grad_self = jnp.dot(inputs.T, masked, preferred_element_type=jnp.float32)
    grad_neigh = jnp.dot(aggregated.T, masked, preferred_element_type=jnp.float32)
    grad_bias = jnp.sum(masked.astype(jnp.float32), axis=0)
    grad_self, grad_neigh, grad_bias = lax.psum((grad_self, grad_neigh, grad_bias), ("row", "col"))
    edge = blocks.shape[1]
    features = strip_grads.shape[1]
    slots = blocks.shape[0]
    turns = 8
    per_turn = slots // turns
    tile_rows = strip_grads.reshape(-1, edge, features)
    strip_tiles = tile_rows.shape[0]
    group_tiles = lax.axis_size("row") * inputs.shape[0] // edge
    live_count = block_count[0, 0]
    offsets = jnp.arange(turns, dtype=jnp.int32) * per_turn
    strip_ids = jnp.arange(strip_tiles, dtype=jnp.int32)
    group_ids = jnp.arange(group_tiles, dtype=jnp.int32)

    def accumulate(partial_value, packed):
        values, row_ids, col_ids, offset = packed
        row_hot = (row_ids[:, None] == strip_ids[None, :]).astype(jnp.bfloat16)
        picked = jnp.einsum(
            "kt,tif->kif", row_hot, tile_rows, preferred_element_type=jnp.float32
        ).astype(jnp.bfloat16)
        product = jnp.einsum("kij,kif->kjf", values, picked, preferred_element_type=jnp.float32)
        active = offset + jnp.arange(per_turn, dtype=jnp.int32) < live_count
        col_hot = ((col_ids[:, None] == group_ids[None, :]) & active[:, None]).astype(jnp.bfloat16)
        upper_part = lax.optimization_barrier(product.astype(jnp.bfloat16))
        remainder = product - upper_part.astype(jnp.float32)
        middle_part = lax.optimization_barrier(remainder.astype(jnp.bfloat16))
        lower_part = (remainder - middle_part.astype(jnp.float32)).astype(jnp.bfloat16)
        added = jnp.einsum("kg,kjf->gjf", col_hot, upper_part, preferred_element_type=jnp.float32)
        added = added + jnp.einsum(
            "kg,kjf->gjf", col_hot, middle_part, preferred_element_type=jnp.float32
        )
        added = added + jnp.einsum(
            "kg,kjf->gjf", col_hot, lower_part, preferred_element_type=jnp.float32
        )
        return (partial_value + added, None)

    partial_value = jnp.zeros((group_tiles, edge, features), jnp.float32)
    partial_value, unused = lax.scan(
        accumulate,
        partial_value,
        (
            blocks.reshape(turns, per_turn, edge, edge),
            block_rows.reshape(turns, per_turn),
            block_cols.reshape(turns, per_turn),
            offsets,
        ),
    )
    neighbour = lax.psum_scatter(
        partial_value.reshape(-1, features).astype(jnp.bfloat16),
        "row",
        scatter_dimension=0,
        tiled=True,
    ).astype(jnp.float32)
    self_term = jnp.dot(masked, w_self.T, preferred_element_type=jnp.float32)
    grad_inputs = (self_term + neighbour).astype(jnp.bfloat16)
    return (grad_inputs, grad_self, grad_neigh, grad_bias)


def solution(mesh):
    return jax.shard_map(
        local,
        mesh=mesh,
        in_specs=(
            P(("row", "col"), None),
            P(("row", "col"), None),
            P(("row", "col"), None),
            P(("row", "col"), None),
            P(("row", "col")),
            P(),
            P(),
            P(("row", "col"), None, None),
            P(("row", "col")),
            P(("row", "col")),
            P("row", "col"),
        ),
        out_specs=(P(("row", "col"), None), P(), P(), P()),
        check_vma=False,
    )
```

profile of v0, /device:TPU:32, one launch (start us, length us, event | category | flops | bytes accessed | tf_op | source)
XLA Modules:
  0.0 424.6 jit_solution(11192621708230141792)
XLA Ops:
  17.1 14.7 %copy.18 = bf16[336,128,128]{1,2,0:T(8,128)(2,1)} copy(bf16[336,128,128]{2,1,0:T(8,128)(2,1)} %param.20) | data formatting | bytes 22020096 | tf_op args[7]
  31.8 23.2 %all-gather.2.cloned.1.call-done = bf16[8192,256]{1,0:T(8,128)(2,1)} async-done(((bf16[512,256]{1,0:T(8,128)(2,1)}), bf16[8192,256]{1,0:T(8,128)(2,1)}) %all-gather.2.cloned.1.call-update) | async-done | bytes 4194320 | tf_op jit(solution)/shard_map/all_gather | solution.py:23
  55.0 256.4 %while.13 = (s32[]{:T(128)}, f32[64,128,256]{2,0,1:T(8,128)}, s32[8,42]{1,0:T(8,128)S(1)}, s32[8]{0:T(128)S(1)}, s32[]{:T(128)}, /*index=5*/bf16[8,42,128,128]{2...) while((s32[]{:T(128)}, f32[64,128,256]{2,0,1:T(8,128)}, ...), condition=%wide.region_1.2_spmd.clone.clone, body=%wide.region_0.1_spmd.clone.clone.sunk | while | flops 1077758464 | bytes 124716728 | solution.py:64
  56.9 5.4 %fusion.64 = bf16[42,128,256]{2,0,1:T(8,128)(2,1)S(1)} fusion(bf16[64,128,256]{2,1,0:T(8,128)(2,1)} %get-tuple-element.242, s32[42]{0:T(128)S(1)} %get-tuple-element.211), kind=kOutput, calls=%fused_computation.5.clone.1 | convolution fusion | flops 176163456 | bytes 6946984 | tf_op jit(solution)/shard_map/while/body/eval_jaxpr/kt,tif->kif/dot_general | solution.py:44
  67.5 3.0 subtract_convert_fusion.2
  75.4 9.4 %select_add_fusion.2 = f32[64,128,256]{2,0,1:T(8,128)} fusion(f32[64,128,256]{2,0,1:T(8,128)} %get-tuple-element.226, f32[64,128,256]{2,0,1:T(8,128)S(1)} %fusion.66, f32[64,128,256]{2,0,1:T(8,128)S(1)} %fusion.68, pred[]{:T(512)S(6)} %compare.3, bf16[42,128,256]{2,1,0:T(8,128)(2,1)} %subtract_convert_fusion.2, s32[42]{0:T(128)S(1)} %get-tuple-element.213, ...), kind=kOutput, calls=%fused_computation.1.clone.1 | convolution fusion | flops 184554752 | bytes 36307156 | tf_op jit(solution)/shard_map/while/body/eval_jaxpr/kg,kjf->gjf/dot_general | solution.py:58
  86.8 5.4 %fusion.64 = bf16[42,128,256]{2,0,1:T(8,128)(2,1)S(1)} fusion(bf16[64,128,256]{2,1,0:T(8,128)(2,1)} %get-tuple-element.242, s32[42]{0:T(128)S(1)} %get-tuple-element.211), kind=kOutput, calls=%fused_computation.5.clone.1 | convolution fusion | flops 176163456 | bytes 6946984 | tf_op jit(solution)/shard_map/while/body/eval_jaxpr/kt,tif->kif/dot_general | solution.py:44
  105.4 11.9 %select_add_fusion.2 = f32[64,128,256]{2,0,1:T(8,128)} fusion(f32[64,128,256]{2,0,1:T(8,128)} %get-tuple-element.226, f32[64,128,256]{2,0,1:T(8,128)S(1)} %fusion.66, f32[64,128,256]{2,0,1:T(8,128)S(1)} %fusion.68, pred[]{:T(512)S(6)} %compare.3, bf16[42,128,256]{2,1,0:T(8,128)(2,1)} %subtract_convert_fusion.2, s32[42]{0:T(128)S(1)} %get-tuple-element.213, ...), kind=kOutput, calls=%fused_computation.1.clone.1 | convolution fusion | flops 184554752 | bytes 36307156 | tf_op jit(solution)/shard_map/while/body/eval_jaxpr/kg,kjf->gjf/dot_general | solution.py:58
  119.2 5.4 %fusion.64 = bf16[42,128,256]{2,0,1:T(8,128)(2,1)S(1)} fusion(bf16[64,128,256]{2,1,0:T(8,128)(2,1)} %get-tuple-element.242, s32[42]{0:T(128)S(1)} %get-tuple-element.211), kind=kOutput, calls=%fused_computation.5.clone.1 | convolution fusion | flops 176163456 | bytes 6946984 | tf_op jit(solution)/shard_map/while/body/eval_jaxpr/kt,tif->kif/dot_general | solution.py:44
  137.7 11.9 %select_add_fusion.2 = f32[64,128,256]{2,0,1:T(8,128)} fusion(f32[64,128,256]{2,0,1:T(8,128)} %get-tuple-element.226, f32[64,128,256]{2,0,1:T(8,128)S(1)} %fusion.66, f32[64,128,256]{2,0,1:T(8,128)S(1)} %fusion.68, pred[]{:T(512)S(6)} %compare.3, bf16[42,128,256]{2,1,0:T(8,128)(2,1)} %subtract_convert_fusion.2, s32[42]{0:T(128)S(1)} %get-tuple-element.213, ...), kind=kOutput, calls=%fused_computation.1.clone.1 | convolution fusion | flops 184554752 | bytes 36307156 | tf_op jit(solution)/shard_map/while/body/eval_jaxpr/kg,kjf->gjf/dot_general | solution.py:58
  151.5 5.4 %fusion.64 = bf16[42,128,256]{2,0,1:T(8,128)(2,1)S(1)} fusion(bf16[64,128,256]{2,1,0:T(8,128)(2,1)} %get-tuple-element.242, s32[42]{0:T(128)S(1)} %get-tuple-element.211), kind=kOutput, calls=%fused_computation.5.clone.1 | convolution fusion | flops 176163456 | bytes 6946984 | tf_op jit(solution)/shard_map/while/body/eval_jaxpr/kt,tif->kif/dot_general | solution.py:44
  170.1 11.9 %select_add_fusion.2 = f32[64,128,256]{2,0,1:T(8,128)} fusion(f32[64,128,256]{2,0,1:T(8,128)} %get-tuple-element.226, f32[64,128,256]{2,0,1:T(8,128)S(1)} %fusion.66, f32[64,128,256]{2,0,1:T(8,128)S(1)} %fusion.68, pred[]{:T(512)S(6)} %compare.3, bf16[42,128,256]{2,1,0:T(8,128)(2,1)} %subtract_convert_fusion.2, s32[42]{0:T(128)S(1)} %get-tuple-element.213, ...), kind=kOutput, calls=%fused_computation.1.clone.1 | convolution fusion | flops 184554752 | bytes 36307156 | tf_op jit(solution)/shard_map/while/body/eval_jaxpr/kg,kjf->gjf/dot_general | solution.py:58
  183.9 5.4 %fusion.64 = bf16[42,128,256]{2,0,1:T(8,128)(2,1)S(1)} fusion(bf16[64,128,256]{2,1,0:T(8,128)(2,1)} %get-tuple-element.242, s32[42]{0:T(128)S(1)} %get-tuple-element.211), kind=kOutput, calls=%fused_computation.5.clone.1 | convolution fusion | flops 176163456 | bytes 6946984 | tf_op jit(solution)/shard_map/while/body/eval_jaxpr/kt,tif->kif/dot_general | solution.py:44
  202.4 11.9 %select_add_fusion.2 = f32[64,128,256]{2,0,1:T(8,128)} fusion(f32[64,128,256]{2,0,1:T(8,128)} %get-tuple-element.226, f32[64,128,256]{2,0,1:T(8,128)S(1)} %fusion.66, f32[64,128,256]{2,0,1:T(8,128)S(1)} %fusion.68, pred[]{:T(512)S(6)} %compare.3, bf16[42,128,256]{2,1,0:T(8,128)(2,1)} %subtract_convert_fusion.2, s32[42]{0:T(128)S(1)} %get-tuple-element.213, ...), kind=kOutput, calls=%fused_computation.1.clone.1 | convolution fusion | flops 184554752 | bytes 36307156 | tf_op jit(solution)/shard_map/while/body/eval_jaxpr/kg,kjf->gjf/dot_general | solution.py:58
  216.2 5.4 %fusion.64 = bf16[42,128,256]{2,0,1:T(8,128)(2,1)S(1)} fusion(bf16[64,128,256]{2,1,0:T(8,128)(2,1)} %get-tuple-element.242, s32[42]{0:T(128)S(1)} %get-tuple-element.211), kind=kOutput, calls=%fused_computation.5.clone.1 | convolution fusion | flops 176163456 | bytes 6946984 | tf_op jit(solution)/shard_map/while/body/eval_jaxpr/kt,tif->kif/dot_general | solution.py:44
  234.7 11.9 %select_add_fusion.2 = f32[64,128,256]{2,0,1:T(8,128)} fusion(f32[64,128,256]{2,0,1:T(8,128)} %get-tuple-element.226, f32[64,128,256]{2,0,1:T(8,128)S(1)} %fusion.66, f32[64,128,256]{2,0,1:T(8,128)S(1)} %fusion.68, pred[]{:T(512)S(6)} %compare.3, bf16[42,128,256]{2,1,0:T(8,128)(2,1)} %subtract_convert_fusion.2, s32[42]{0:T(128)S(1)} %get-tuple-element.213, ...), kind=kOutput, calls=%fused_computation.1.clone.1 | convolution fusion | flops 184554752 | bytes 36307156 | tf_op jit(solution)/shard_map/while/body/eval_jaxpr/kg,kjf->gjf/dot_general | solution.py:58
  248.5 5.4 %fusion.64 = bf16[42,128,256]{2,0,1:T(8,128)(2,1)S(1)} fusion(bf16[64,128,256]{2,1,0:T(8,128)(2,1)} %get-tuple-element.242, s32[42]{0:T(128)S(1)} %get-tuple-element.211), kind=kOutput, calls=%fused_computation.5.clone.1 | convolution fusion | flops 176163456 | bytes 6946984 | tf_op jit(solution)/shard_map/while/body/eval_jaxpr/kt,tif->kif/dot_general | solution.py:44
  267.1 11.9 %select_add_fusion.2 = f32[64,128,256]{2,0,1:T(8,128)} fusion(f32[64,128,256]{2,0,1:T(8,128)} %get-tuple-element.226, f32[64,128,256]{2,0,1:T(8,128)S(1)} %fusion.66, f32[64,128,256]{2,0,1:T(8,128)S(1)} %fusion.68, pred[]{:T(512)S(6)} %compare.3, bf16[42,128,256]{2,1,0:T(8,128)(2,1)} %subtract_convert_fusion.2, s32[42]{0:T(128)S(1)} %get-tuple-element.213, ...), kind=kOutput, calls=%fused_computation.1.clone.1 | convolution fusion | flops 184554752 | bytes 36307156 | tf_op jit(solution)/shard_map/while/body/eval_jaxpr/kg,kjf->gjf/dot_general | solution.py:58
  280.9 5.4 %fusion.64 = bf16[42,128,256]{2,0,1:T(8,128)(2,1)S(1)} fusion(bf16[64,128,256]{2,1,0:T(8,128)(2,1)} %get-tuple-element.242, s32[42]{0:T(128)S(1)} %get-tuple-element.211), kind=kOutput, calls=%fused_computation.5.clone.1 | convolution fusion | flops 176163456 | bytes 6946984 | tf_op jit(solution)/shard_map/while/body/eval_jaxpr/kt,tif->kif/dot_general | solution.py:44
  299.4 11.9 %select_add_fusion.2 = f32[64,128,256]{2,0,1:T(8,128)} fusion(f32[64,128,256]{2,0,1:T(8,128)} %get-tuple-element.226, f32[64,128,256]{2,0,1:T(8,128)S(1)} %fusion.66, f32[64,128,256]{2,0,1:T(8,128)S(1)} %fusion.68, pred[]{:T(512)S(6)} %compare.3, bf16[42,128,256]{2,1,0:T(8,128)(2,1)} %subtract_convert_fusion.2, s32[42]{0:T(128)S(1)} %get-tuple-element.213, ...), kind=kOutput, calls=%fused_computation.1.clone.1 | convolution fusion | flops 184554752 | bytes 36307156 | tf_op jit(solution)/shard_map/while/body/eval_jaxpr/kg,kjf->gjf/dot_general | solution.py:58
  311.3 4.0 convert_element_type.51
  315.4 4.4 %copy.19 = bf16[64,128,256]{2,1,0:T(8,128)(2,1)} copy(bf16[64,128,256]{2,0,1:T(8,128)(2,1)S(1)} %convert_element_type.51) | data formatting | bytes 8388608 | tf_op jit(solution)/shard_map/convert_element_type | solution.py:75
  320.4 78.5 %psum.23 = f32[256]{0:T(256)} all-reduce(f32[256]{0:T(256)S(1)} %copy-done.7), channel_id=1, replica_groups=mesh['row'=16,'col'=16] {'row','col'}, use_global_device_ids=true, to_apply=%region_6.7 | all-reduce | flops 256 | bytes 2048 | tf_op jit(solution)/shard_map/psum | solution.py:27
  402.6 12.7 %reduce-scatter.2.cloned.1.call-done = bf16[512,256]{1,0:T(8,128)(2,1)} async-done(((bf16[8192,256]{1,0:T(8,128)(2,1)}), bf16[512,256]{1,0:T(8,128)(2,1)}) %reduce-scatter.2.cloned.1.call-update) | async-done | bytes 262160 | tf_op jit(solution)/shard_map/reduce_scatter | solution.py:74
  (126 shorter events, 132.1 us)
Async XLA Ops:
  8.0 4.5 %copy-start = (bf16[512,256]{1,0:T(8,128)(2,1)S(1)}, bf16[512,256]{1,0:T(8,128)(2,1)}, u32[]{:S(2)}) copy-start(bf16[512,256]{1,0:T(8,128)(2,1)} %param.14) | copy-start | bytes 786436
  8.0 47.0 %all-gather.2.cloned.1.call-start = ((), (), s32[]{:S(2)}) async-start(), calls=%async_computation.1 | async-start | bytes 4456448 | tf_op jit(solution)/shard_map/all_gather | solution.py:23
  10.5 21.3 %copy-start.4 = (bf16[512,256]{1,0:T(8,128)(2,1)}, bf16[512,256]{1,0:T(8,128)(2,1)S(1)}, u32[]{:S(2)}) copy-start(bf16[512,256]{1,0:T(8,128)(2,1)S(1)} %get-tuple-element.153) | copy-start | bytes 786436
  12.5 386.5 %all-reduce.3.cloned.1.call-start = ((), (), s32[]{:S(2)}) async-start(), calls=%async_computation.3 | async-start | bytes 1048576 | tf_op jit(solution)/shard_map/psum | solution.py:27
  15.5 399.7 %reduce-scatter.2.cloned.1.call-start = ((), (), s32[]{:S(2)}) async-start(), calls=%async_computation.2 | async-start | bytes 4456448 | tf_op jit(solution)/shard_map/reduce_scatter | solution.py:74
  65.9 1.5 copy-start.2
  70.5 2.5 copy-start.3
  95.8 1.5 copy-start.2
  100.4 2.5 copy-start.3
  128.2 1.5 copy-start.2
  132.7 2.5 copy-start.3
  160.6 1.5 copy-start.2
  165.1 2.5 copy-start.3
  192.9 1.5 copy-start.2
  197.4 2.5 copy-start.3
  225.2 1.5 copy-start.2
  229.8 2.5 copy-start.3
  257.6 1.5 copy-start.2
  262.1 2.5 copy-start.3
  289.9 1.5 copy-start.2
  294.5 2.5 copy-start.3
  315.4 101.8 %copy-start.1 = (bf16[512,256]{1,0:T(8,128)(2,1)S(1)}, bf16[512,256]{1,0:T(8,128)(2,1)}, u32[]{:S(2)}) copy-start(bf16[512,256]{1,0:T(8,128)(2,1)} %param.14) | copy-start | bytes 786436
  319.8 95.5 %copy-start.5 = (bf16[512,256]{1,0:T(8,128)(2,1)S(1)}, bf16[512,256]{1,0:T(8,128)(2,1)}, u32[]{:S(2)}) copy-start(bf16[512,256]{1,0:T(8,128)(2,1)} %copy-done.4) | copy-start | bytes 786436
  319.8 95.5 %copy-start.6 = (bf16[256,256]{1,0:T(8,128)(2,1)S(1)}, bf16[256,256]{1,0:T(8,128)(2,1)}, u32[]{:S(2)}) copy-start(bf16[256,256]{1,0:T(8,128)(2,1)} %param.18) | copy-start | bytes 393220
  (1 other events, 0.7 us)
Sparse Core Ops, SparseCore 0:
  12.6 42.3 all-gather.1
  319.9 95.2 reduce-scatter.1
Sparse Core Ops, SparseCore 1:
  20.1 252.6 all-reduce.2
where the time goes:
time: 428 us; the launch traced here: 425 us
  matrix products  203 us (47%)
  blocking collectives  78.5 us (18%)
  other arithmetic  49.1 us (11%)
  local copies, waits for them, and re-layouts  41.6 us (10%)
  waiting for transfers between devices  35.9 us (8%)
  between operations  15.5 us (4%)
    dot_general x8, matrix products, accumulate(): jnp.einsum('kg,kjf->gjf', col_hot, lower_part, preferred_element_type=jnp...  92.7 us
    psum x1, blocking collectives, local(): lax.psum((grad_self, grad_neigh, grad_bias), ('row', 'col'))  78.5 us
    dot_general x8, matrix products, accumulate(): jnp.einsum('kt,tif->kif', row_hot, tile_rows, preferred_element_type=jnp....  43.3 us
    convert_element_type x8, other arithmetic, accumulate(): (remainder - middle_part.astype(jnp.float32)).astype(jnp.bfloat16)  24.1 us
    all_gather x1, waiting for transfers between devices, local(): strip_grads = lax.all_gather(local_grads, 'col', axis=0, tiled=True)  23.2 us
    dot_general x8, matrix products, accumulate(): jnp.einsum('kij,kif->kjf', values, picked, preferred_element_type=jnp.flo...  20.9 us
    dot_general x8, matrix products, accumulate(): jnp.einsum('kg,kjf->gjf', col_hot, middle_part, preferred_element_type=jn...  19.9 us
    dot_general x8, matrix products, accumulate(): jnp.einsum('kg,kjf->gjf', col_hot, upper_part, preferred_element_type=jnp...  19.7 us
  transfers between devices with their start and end apart: 3, of which 2 were waited for; matrix products, arithmetic and copies ran while one was open for 65% of the time, Pallas kernels for 0%

commit v1 on v0

v1 whole, which is shorter than its diff:
```python
import functools

import jax
import jax.numpy as jnp
from jax import lax
from jax.experimental import pallas as pl
from jax.experimental.pallas import tpu as pltpu
from jax.sharding import PartitionSpec as P

EDGE = 128
F32 = jnp.float32
BF16 = jnp.bfloat16
FLOWS = (("y", "z", 0, 384), ("z", "y", 384, 128))
SHARE = 32
SHARE_PAD = 40


def place():
    r = lax.axis_index("row")
    c = lax.axis_index("col")
    return r // 4, r % 4, c // 4, (c // 2) % 2, c % 2


def device(y, z, x, pair, core):
    return {"row": y * 4 + z, "col": x * 4 + pair * 2 + core}


def greet(peers):
    barrier = pltpu.get_barrier_semaphore()
    for peer in peers:
        pl.semaphore_signal(barrier, inc=1, device_id=peer, device_id_type=pl.DeviceIdType.MESH)
    pl.semaphore_wait(barrier, len(peers))


class Post:
    def __init__(self, send_sem, recv_sem):
        self.send_sem = send_sem
        self.recv_sem = recv_sem
        self.sent = []

    def send(self, src, dst, peer):
        at = len(self.sent)
        copy = pltpu.make_async_remote_copy(
            src_ref=src,
            dst_ref=dst,
            send_sem=self.send_sem.at[at],
            recv_sem=self.recv_sem.at[at],
            device_id=peer,
            device_id_type=pl.DeviceIdType.MESH,
        )
        copy.start()
        self.sent.append(copy)
        return copy

    def finish(self):
        for copy in self.sent:
            copy.wait_send()


def gather_kernel(
    inputs, aggregated, grad_out, preact, inv, w_self, w_neigh,
    strip_out, self_term, shares, strip, masked_ref, send_sem, recv_sem, out_sem,
):
    y, z, x, pair, core = place()
    rows = inputs.shape[0]
    half = rows // 2
    right, left, opposite, other = (x + 1) % 4, (x + 3) % 4, (x + 2) % 4, 1 - pair
    to_right = device(y, z, right, pair, core)
    to_left = device(y, z, left, pair, core)
    to_pair = device(y, z, x, other, core)
    to_core = device(y, z, x, pair, 1 - core)
    greet((to_right, to_left, to_pair, to_core))
    post = Post(send_sem, recv_sem)
    stored = []

    def part(at_x, at_pair, at_core, h):
        shard = (at_x * 2 + at_pair) * 2 + at_core
        return pl.ds(pl.multiple_of(shard * rows + h * half, half), half)

    def send(where, peer):
        return post.send(strip.at[where], strip.at[where], peer)

    def store(where):
        copy = pltpu.make_async_copy(strip.at[where], strip_out.at[where], out_sem.at[len(stored)])
        copy.start()
        stored.append(copy)

    eye = lax.broadcasted_iota(jnp.int32, (EDGE, EDGE), 0) == lax.broadcasted_iota(
        jnp.int32, (EDGE, EDGE), 1
    )
    own_right, own_left, own_pair, own_core = {}, {}, {}, {}
    for h in range(2):
        base = h * half
        grads = grad_out[base : base + half, :]
        masked = jnp.where(preact[base : base + half, :] > 0, grads, jnp.zeros_like(grads))
        masked_ref[base : base + half, :] = masked
        projected = lax.dot_general(
            masked, w_neigh[...], (((1,), (1,)), ((), ())), preferred_element_type=F32
        )
        for t in range(half // EDGE):
            at = h * (half // EDGE) + t
            row = jnp.broadcast_to(inv[at : at + 1, :], (EDGE, EDGE))
            scale = jnp.sum(jnp.where(eye, row, jnp.zeros_like(row)), axis=1, keepdims=True)
            shard = (x * 2 + pair) * 2 + core
            place_at = pl.ds(pl.multiple_of(shard * rows + at * EDGE, EDGE), EDGE)
            strip[place_at, :] = (projected[t * EDGE : (t + 1) * EDGE, :] * scale).astype(BF16)
        mine = part(x, pair, core, h)
        own_right[h] = send(mine, to_right)
        own_left[h] = send(mine, to_left)
        own_pair[h] = send(mine, to_pair)
        own_core[h] = send(mine, to_core)
        store(mine)

    masked = masked_ref[...]
    self_term[...] = lax.dot_general(
        masked, w_self[...], (((1,), (1,)), ((), ())), preferred_element_type=F32
    )
    bias = jnp.sum(masked.astype(F32), axis=0, keepdims=True)
    count = shares.shape[0] // 2
    for which, left_side in enumerate((inputs, aggregated)):
        product = lax.dot_general(
            left_side[...], masked, (((0,), (0,)), ((), ())), preferred_element_type=F32
        )
        for q in range(count):
            shares[which * count + q, :SHARE, :] = product[q * SHARE : (q + 1) * SHARE, :]
            shares[which * count + q, SHARE:, :] = jnp.broadcast_to(
                bias, (SHARE_PAD - SHARE, bias.shape[1])
            )

    passed = []

    def arrived(copy, spot):
        copy.wait_recv()
        at_x, at_pair, h = spot
        where = part(at_x, at_pair, core, h)
        passed.append((send(where, to_core), part(at_x, at_pair, 1 - core, h)))
        store(where)
        return where

    for h in range(2):
        passed.append((own_core[h], part(x, pair, 1 - core, h)))
    where = arrived(own_right[0], (left, pair, 0))
    far_0 = send(where, to_right)
    where = arrived(own_left[0], (right, pair, 0))
    where = arrived(own_pair[0], (x, other, 0))
    other_right_0 = send(where, to_right)
    other_left_0 = send(where, to_left)
    where = arrived(own_left[1], (right, pair, 1))
    far_1 = send(where, to_left)
    where = arrived(own_right[1], (left, pair, 1))
    where = arrived(own_pair[1], (x, other, 1))
    other_right_1 = send(where, to_right)
    other_left_1 = send(where, to_left)
    where = arrived(far_0, (opposite, pair, 0))
    far_pair_0 = send(where, to_pair)
    where = arrived(far_1, (opposite, pair, 1))
    far_pair_1 = send(where, to_pair)
    arrived(other_right_0, (left, other, 0))
    arrived(other_left_0, (right, other, 0))
    arrived(other_right_1, (left, other, 1))
    arrived(other_left_1, (right, other, 1))
    arrived(far_pair_0, (opposite, other, 0))
    arrived(far_pair_1, (opposite, other, 1))
    for copy, where in passed:
        copy.wait_recv()
        store(where)
    for copy in stored:
        copy.wait()
    post.finish()


def spmm_kernel(
    rows_ref, cols_ref, count_ref, blocks, strip_in, out, strip, total, ring, ring_sem, strip_sem
):
    depth, chunk = ring.shape[0], ring.shape[1]
    group = 16
    live_count = count_ref[0]
    chunks = lax.div(live_count + chunk - 1, chunk)
    strip_copy = pltpu.make_async_copy(strip_in, strip, strip_sem)
    strip_copy.start()

    def fetch(at, slot):
        return pltpu.make_async_copy(
            blocks.at[pl.ds(at * chunk, chunk)], ring.at[slot], ring_sem.at[slot]
        )

    for at in range(depth - 1):

        @pl.when(at < chunks)
        def _():
            fetch(at, at).start()

    tall = 256

    def clear(t, carry):
        total[pl.ds(pl.multiple_of(t * tall, tall), tall), :] = jnp.zeros(
            (tall, total.shape[1]), F32
        )
        return carry

    lax.fori_loop(0, total.shape[0] // tall, clear, 0)
    strip_copy.wait()

    def one(at, slot, inner):
        r = pl.multiple_of(rows_ref[at] * EDGE, EDGE)
        c = pl.multiple_of(cols_ref[at] * EDGE, EDGE)
        total[pl.ds(c, EDGE), :] += lax.dot_general(
            ring[slot, inner],
            strip[pl.ds(r, EDGE), :],
            (((0,), (0,)), ((), ())),
            preferred_element_type=F32,
        )

    def step(at, carry):
        slot = lax.rem(at, depth)
        ahead = at + depth - 1

        @pl.when(ahead < chunks)
        def _():
            fetch(ahead, lax.rem(ahead, depth)).start()

        fetch(at, slot).wait()
        live = jnp.minimum(live_count - at * chunk, chunk)
        groups = lax.div(live, group)

        def many(u, carry):
            for i in range(group):
                one(at * chunk + u * group + i, slot, u * group + i)
            return carry

        lax.fori_loop(0, groups, many, 0)

        def rest(i, carry):
            one(at * chunk + i, slot, i)
            return carry

        lax.fori_loop(groups * group, live, rest, 0)
        return carry

    lax.fori_loop(0, chunks, step, 0)

    def leave(t, carry):
        span = pl.ds(pl.multiple_of(t * tall, tall), tall)
        out[span, :] = total[span, :].astype(BF16)
        return carry

    lax.fori_loop(0, total.shape[0] // tall, leave, 0)


def reduce_kernel(partial, self_term, shares, out, weights, bias, *scratch):
    flow_refs = [scratch[i * 7 : i * 7 + 7] for i in range(len(FLOWS))]
    from_core, from_pair, from_x, from_y, from_z, work_a, work_b, work_c, work_d, work_e = scratch[14:24]
    send_sem, recv_sem = scratch[24:26]
    y, z, x, pair, core = place()
    rows = self_term.shape[0]
    turn = lambda v, by: (v + by) % 4
    peer_y = {by: device(turn(y, by), z, x, pair, core) for by in (1, 2, 3)}
    peer_z = {by: device(y, turn(z, by), x, pair, core) for by in (1, 2, 3)}
    peer_x = {by: device(y, z, turn(x, by), pair, core) for by in (1, 2, 3)}
    to_pair = device(y, z, x, 1 - pair, core)
    to_core = device(y, z, x, pair, 1 - core)
    greet(
        [peer[by] for peer in (peer_y, peer_z, peer_x) for by in (1, 2, 3)] + [to_pair, to_core]
    )
    post = Post(send_sem, recv_sem)
    peers = {"y": peer_y, "z": peer_z}
    own = {"y": y, "z": z}

    def flow(refs, first, second, offset, span):
        via_a, left_a, right_a, sum_a, hold, via_b, side_b = refs
        h = span // 2
        halves = (slice(0, h), slice(h, span))
        ahead_a, back_a = peers[first][1], peers[first][3]
        ahead_b, back_b = peers[second][1], peers[second][3]
        order = (2, 1, 3, 0)

        def piece(by_a, by_b, k):
            at = {first: turn(own[first], by_a), second: turn(own[second], by_b)}
            start = (at["y"] * 4 + at["z"]) * rows + offset
            if k is None:
                return pl.ds(pl.multiple_of(start, 16), span)
            return pl.ds(pl.multiple_of(start + k * h, 16), h)

        far, near = {}, {}

        def launch(i):
            b = order[i]
            far[i] = (
                post.send(partial.at[piece(2, b, 0)], via_a.at[i, 0], ahead_a),
                post.send(partial.at[piece(2, b, 1)], via_a.at[i, 1], back_a),
            )
            near[i] = [
                post.send(partial.at[piece(1, b, 1)], left_a.at[i, pl.ds(h, h)], ahead_a),
                post.send(partial.at[piece(3, b, 0)], right_a.at[i, pl.ds(0, h)], back_a),
            ]

        def relay(i):
            b = order[i]
            far[i][0].wait_recv()
            sum_a[i, 0] = (
                via_a[i, 0].astype(F32) + partial[piece(1, b, 0), :].astype(F32)
            ).astype(BF16)
            near[i].append(post.send(sum_a.at[i, 0], left_a.at[i, pl.ds(0, h)], ahead_a))
            far[i][1].wait_recv()
            sum_a[i, 1] = (
                via_a[i, 1].astype(F32) + partial[piece(3, b, 1), :].astype(F32)
            ).astype(BF16)
            near[i].append(post.send(sum_a.at[i, 1], right_a.at[i, pl.ds(h, h)], back_a))

        def close(i):
            for copy in near[i]:
                copy.wait_recv()
            return (
                partial[piece(0, order[i], None), :].astype(F32)
                + left_a[i].astype(F32)
                + right_a[i].astype(F32)
            )

        launch(0)
        launch(1)
        yield
        sent_b = []
        for i in range(5):
            if i < 4:
                relay(i)
                if i + 2 < 4:
                    launch(i + 2)
                yield
            if i == 0:
                continue
            done = close(i - 1)
            if i == 1:
                hold[0] = done.astype(BF16)
                far_b = (
                    post.send(hold.at[0, pl.ds(0, h)], via_b.at[0], ahead_b),
                    post.send(hold.at[0, pl.ds(h, h)], via_b.at[1], back_b),
                )
            elif i == 2:
                hold[1, pl.ds(h, h), :] = done[halves[1], :].astype(BF16)
                sent_b.append(
                    post.send(hold.at[1, pl.ds(h, h)], side_b.at[0, pl.ds(h, h)], ahead_b)
                )
                far_b[0].wait_recv()
                hold[1, pl.ds(0, h), :] = (done[halves[0], :] + via_b[0].astype(F32)).astype(BF16)
                sent_b.append(
                    post.send(hold.at[1, pl.ds(0, h)], side_b.at[0, pl.ds(0, h)], ahead_b)
                )
            elif i == 3:
                hold[2, pl.ds(0, h), :] = done[halves[0], :].astype(BF16)
                sent_b.append(
                    post.send(hold.at[2, pl.ds(0, h)], side_b.at[1, pl.ds(0, h)], back_b)
                )
                far_b[1].wait_recv()
                hold[2, pl.ds(h, h), :] = (done[halves[1], :] + via_b[1].astype(F32)).astype(BF16)
                sent_b.append(
                    post.send(hold.at[2, pl.ds(h, h)], side_b.at[1, pl.ds(h, h)], back_b)
                )
            else:
                done = done + self_term[pl.ds(offset, span), :]
                yield
                for copy in sent_b:
                    copy.wait_recv()
                out[pl.ds(offset, span), :] = (
                    done + side_b[0].astype(F32) + side_b[1].astype(F32)
                ).astype(BF16)
            yield

    def weight_sums():
        eight, four = shares.shape[0] // 2, shares.shape[0] // 4
        copy = post.send(shares.at[pl.ds((1 - core) * eight, eight)], from_core, to_core)
        yield
        copy.wait_recv()
        work_a[...] = shares[pl.ds(core * eight, eight)] + from_core[...]
        copy = post.send(work_a.at[pl.ds((1 - pair) * four, four)], from_pair, to_pair)
        yield
        copy.wait_recv()
        work_b[...] = work_a[pl.ds(pair * four, four)] + from_pair[...]
        copies = [
            post.send(work_b.at[turn(x, by)], from_x.at[by - 1], peer_x[by]) for by in (1, 2, 3)
        ]
        yield
        for copy in copies:
            copy.wait_recv()
        work_c[...] = work_b[x] + from_x[0] + from_x[1] + from_x[2]
        from_y[y] = work_c[...]
        copies = [post.send(work_c, from_y.at[y], peer_y[by]) for by in (1, 2, 3)]
        yield
        for copy in copies:
            copy.wait_recv()
        work_d[...] = from_y[0] + from_y[1] + from_y[2] + from_y[3]
        from_z[z] = work_d[...]
        copies = [post.send(work_d, from_z.at[z], peer_z[by]) for by in (1, 2, 3)]
        yield
        for copy in copies:
            copy.wait_recv()
        work_e[...] = from_z[0] + from_z[1] + from_z[2] + from_z[3]
        bias[...] = work_e[pl.ds(SHARE, SHARE_PAD - SHARE), :]
        mine = core * eight + pair * four + x

        def span(first, count):
            return pl.ds(pl.multiple_of(first * SHARE, SHARE), count * SHARE)

        weights[span(mine, 1), :] = work_e[pl.ds(0, SHARE), :]
        copies = [
            post.send(work_e.at[pl.ds(0, SHARE)], weights.at[span(mine, 1)], peer_x[by])
            for by in (1, 2, 3)
        ]
        yield
        for copy in copies:
            copy.wait_recv()
        where = span(core * eight + pair * four, four)
        copy = post.send(weights.at[where], weights.at[where], to_pair)
        yield
        copy.wait_recv()
        where = span(core * eight, eight)
        copy = post.send(weights.at[where], weights.at[where], to_core)
        yield
        copy.wait_recv()

    turns = [flow(refs, *spec) for refs, spec in zip(flow_refs, FLOWS)] + [weight_sums()]
    while turns:
        for one in list(turns):
            try:
                next(one)
            except StopIteration:
                turns.remove(one)
    post.finish()


def local(
    inputs, aggregated, grad_out, preact, inv_degree, w_self, w_neigh,
    blocks, block_rows, block_cols, block_count,
):
    rows, feat = inputs.shape
    strip_rows = rows * lax.axis_size("col")
    group_rows = rows * lax.axis_size("row")
    vmem = pl.BlockSpec(memory_space=pltpu.VMEM)
    anywhere = pl.BlockSpec(memory_space=pl.ANY)
    dma = pltpu.SemaphoreType.DMA
    inv = inv_degree.astype(F32).reshape(rows // EDGE, EDGE)
    strip, self_term, shares = pl.pallas_call(
        gather_kernel,
        out_shape=(
            jax.ShapeDtypeStruct((strip_rows, feat), BF16),
            jax.ShapeDtypeStruct((rows, feat), F32),
            jax.ShapeDtypeStruct((16, SHARE_PAD, feat), F32),
        ),
        in_specs=[vmem] * 7,
        out_specs=(anywhere, vmem, vmem),
        scratch_shapes=[
            pltpu.VMEM((strip_rows, feat), BF16),
            pltpu.VMEM((rows, feat), BF16),
            dma((30,)),
            dma((30,)),
            dma((32,)),
        ],
        compiler_params=pltpu.CompilerParams(
            collective_id=0, has_side_effects=True, vmem_limit_bytes=32 * 2**20
        ),
        name="gather",
    )(inputs, aggregated, grad_out, preact, inv, w_self, w_neigh)

    depth, chunk = 4, 16
    partial = pl.pallas_call(
        spmm_kernel,
        out_shape=jax.ShapeDtypeStruct((group_rows, feat), BF16),
        grid_spec=pltpu.PrefetchScalarGridSpec(
            num_scalar_prefetch=3,
            grid=(1,),
            in_specs=[anywhere, anywhere],
            out_specs=pl.BlockSpec((group_rows, feat), lambda i, *unused: (0, 0)),
            scratch_shapes=[
                pltpu.VMEM((strip_rows, feat), BF16),
                pltpu.VMEM((group_rows, feat), F32),
                pltpu.VMEM((depth, chunk, EDGE, EDGE), BF16),
                dma((depth,)),
                dma,
            ],
        ),
        compiler_params=pltpu.CompilerParams(vmem_limit_bytes=40 * 2**20),
        name="spmm",
    )(block_rows, block_cols, block_count.reshape(1), blocks, strip)

    scratch = []
    for unused_a, unused_b, unused_c, span in FLOWS:
        scratch += [
            pltpu.VMEM((4, 2, span // 2, feat), BF16),
            pltpu.VMEM((4, span, feat), BF16),
            pltpu.VMEM((4, span, feat), BF16),
            pltpu.VMEM((4, 2, span // 2, feat), BF16),
            pltpu.VMEM((3, span, feat), BF16),
            pltpu.VMEM((2, span // 2, feat), BF16),
            pltpu.VMEM((2, span, feat), BF16),
        ]
    share = (SHARE_PAD, feat)
    scratch += [
        pltpu.VMEM((8,) + share, F32),
        pltpu.VMEM((4,) + share, F32),
        pltpu.VMEM((3,) + share, F32),
        pltpu.VMEM((4,) + share, F32),
        pltpu.VMEM((4,) + share, F32),
        pltpu.VMEM((8,) + share, F32),
        pltpu.VMEM((4,) + share, F32),
        pltpu.VMEM(share, F32),
        pltpu.VMEM(share, F32),
        pltpu.VMEM(share, F32),
        dma((2 * 30 + 16,)),
        dma((2 * 30 + 16,)),
    ]
    grad_inputs, weights, bias = pl.pallas_call(
        reduce_kernel,
        out_shape=(
            jax.ShapeDtypeStruct((rows, feat), BF16),
            jax.ShapeDtypeStruct((16 * SHARE, feat), F32),
            jax.ShapeDtypeStruct((SHARE_PAD - SHARE, feat), F32),
        ),
        in_specs=[vmem] * 3,
        out_specs=(vmem, vmem, vmem),
        scratch_shapes=scratch,
        compiler_params=pltpu.CompilerParams(
            collective_id=1, has_side_effects=True, vmem_limit_bytes=32 * 2**20
        ),
        name="reduce",
    )(partial, self_term, shares)
    return grad_inputs, weights[:feat], weights[feat:], bias[0]


def solution(mesh):
    both = ("row", "col")
    return jax.shard_map(
        local,
        mesh=mesh,
        in_specs=(
            P(both, None), P(both, None), P(both, None), P(both, None), P(both),
            P(), P(),
            P(both, None, None), P(both), P(both), P("row", "col"),
        ),
        out_specs=(P(both, None), P(), P(), P()),
        check_vma=False,
    )
```

time: 428 us -> 105 us (0.25)
  matrix products: 203 us -> 0 us
  Pallas kernels: 0 us -> 92.7 us
  blocking collectives: 78.5 us -> 0 us
  other arithmetic: 49.1 us -> 0.68 us
  waiting for transfers between devices: 35.9 us -> 0 us
  local copies, waits for them, and re-layouts: 41.6 us -> 9.05 us
  between operations: 15.5 us -> 1.32 us
    dot_general x44 -> x0, matrix products: 203 us -> none  [the longest x8 92.7 us: accumulate(): jnp.einsum('kg,kjf->gjf', col_hot, lower_part, preferred_element_type=jnp...]
    pallas_call x0 -> x3, Pallas kernels: none -> 92.7 us  [the longest x1 63.5 us: local(): pl.pallas_call(reduce_kernel, out_shape=(jax.ShapeDtypeStruct((rows, feat...]
    psum x1 -> x0, blocking collectives: 78.5 us -> none  [local(): lax.psum((grad_self, grad_neigh, grad_bias), ('row', 'col'))]
    convert_element_type x18 -> x0, other arithmetic: 37 us -> none  [the longest x8 24.1 us: accumulate(): (remainder - middle_part.astype(jnp.float32)).astype(jnp.bfloat16)]
    all_gather x1 -> x0, waiting for transfers between devices: 23.2 us -> none  [local(): strip_grads = lax.all_gather(local_grads, 'col', axis=0, tiled=True)]
    reduce_scatter x1 -> x0, waiting for transfers between devices: 12.7 us -> none  [local(): lax.psum_scatter(partial_value.reshape(-1, features).astype(jnp.bfloat16)...]
    while x32 -> x0, local copies, waits for them, and re-layouts: 12 us -> none
    unnamed x15 -> x17, local copies, waits for them, and re-layouts: 19 us -> 7.67 us
  transfers between devices with their start and end apart: 3 -> 0, of which waited for: 2 -> 0; matrix products, arithmetic and copies ran while one was open for 65% -> 0% of each run, Pallas kernels for 0% -> 0%
where the time goes in v1:
time: 105 us; the launch traced here: 104 us
  Pallas kernels  92.7 us (88%)
  local copies, waits for them, and re-layouts  9.05 us (9%)
  between operations  1.32 us (1%)
    pallas_call x1, Pallas kernels, local(): pl.pallas_call(reduce_kernel, out_shape=(jax.ShapeDtypeStruct((rows, feat...  63.5 us
    pallas_call x1, Pallas kernels, local(): pl.pallas_call(gather_kernel, out_shape=(jax.ShapeDtypeStruct((strip_rows...  23.7 us
    unnamed x17, local copies, waits for them, and re-layouts  7.67 us
    pallas_call x1, Pallas kernels, local(): pl.pallas_call(spmm_kernel, out_shape=jax.ShapeDtypeStruct((group_rows, f...  5.45 us

profile of v1, /device:TPU:32, one launch (start us, length us, event | category | flops | bytes accessed | tf_op | source)
XLA Modules:
  0.0 103.7 jit_solution(17360418491272107806)
XLA Ops:
  1.3 0.7 bitcast_convert_fusion.inv
  2.0 0.0 copy-start
  2.0 0.9 copy-done
  2.9 0.0 copy-start.1
  2.9 0.9 copy-done.1
  3.9 0.0 copy-start.2
  3.9 0.9 copy-done.2
  4.8 0.0 copy-start.3
  4.8 0.9 copy-done.3
  5.8 0.0 copy-start.4
  5.8 0.9 copy-done.4
  6.7 0.0 copy-start.5
  6.7 0.9 copy-done.5
  7.6 23.7 %gather.1 = (bf16[8192,256]{1,0:T(8,128)(2,1)S(1)}, f32[512,256]{1,0:T(8,128)S(1)}, f32[16,40,256]{2,1,0:T(8,128)S(1)}) custom-call(bf16[512,256]{1,0:T(8,128)(2,1)S(1)} %copy-done, bf16[512,256]{1,0:T(8,128)(2,1)S(1)} %copy-done.1, bf16[512,256]{1,0:T(8,128)(2,1)S(1)} %copy-done.2, bf16[512,256]{1,0:T(8,128)(2,1)S(1)} %copy-done.3, ...), custom_call_target="tpu_custom_call" | custom-call | tf_op jit(solution)/shard_map/gather/pallas_call | solution.py:441
  31.3 0.0 copy-start.6
  31.3 0.7 copy-done.6
  32.0 0.0 copy-start.7
  32.0 0.7 copy-done.7
  32.6 5.4 %spmm.1.partial = bf16[8192,256]{1,0:T(8,128)(2,1)S(1)} custom-call(s32[336]{0:T(512)S(1)} %copy-done.6, s32[336]{0:T(512)S(1)} %copy-done.7, s32[1]{0:T(128)} %bitcast.5.count_ref, bf16[336,128,128]{2,1,0:T(8,128)(2,1)} %blocks.1, bf16[8192,256]{1,0:T(8,128)(2,1)S(1)} %get-tuple-element.10.strip_in), custom_call_target="tpu_custom_call" | custom-call | tf_op jit(solution)/shard_map/spmm/pallas_call | solution.py:464
  38.1 63.5 %reduce.1 = (bf16[512,256]{1,0:T(8,128)(2,1)S(1)}, f32[512,256]{1,0:T(8,128)S(1)}, f32[8,256]{1,0:T(8,128)S(1)}) custom-call(bf16[8192,256]{1,0:T(8,128)(2,1)S(1)} %spmm.1.partial, f32[512,256]{1,0:T(8,128)S(1)} %get-tuple-element.11.self_term, f32[16,40,256]{2,1,0:T(8,128)S(1)} %get-tuple-element.12.shares), custom_call_target="tpu_custom_call" | custom-call | tf_op jit(solution)/shard_map/reduce/pallas_call | solution.py:510
  101.6 0.6 slice.11
  102.2 0.8 fusion
  103.0 0.7 copy.17
Async XLA Ops:
  2.0 0.9 copy-start
  2.9 0.9 copy-start.1
  3.9 0.9 copy-start.2
  4.8 0.9 copy-start.3
  5.8 0.9 copy-start.4
  6.7 0.9 copy-start.5
  31.3 0.7 copy-start.6
  32.0 0.7 copy-start.7

commit v2 on v0

v2 whole, which is shorter than its diff:
```python
import functools

import jax
import jax.numpy as jnp
from jax import lax
from jax.experimental import pallas as pl
from jax.experimental.pallas import tpu as pltpu
from jax.sharding import PartitionSpec as P

EDGE = 128
HALVES = 2
TILES = 64
I32 = jnp.int32
F32 = jnp.float32
BF16 = jnp.bfloat16
FLOWS = (("y", "z", 0, 384), ("z", "y", 384, 128))
PAD = 8
LIMIT = 62
PAIRS = 200
STRIDE = 20
PART = 40


def place():
    r = lax.axis_index("row")
    c = lax.axis_index("col")
    return r // 4, r % 4, c // 4, (c // 2) % 2, c % 2


def device(y, z, x, pair, core):
    return {"row": y * 4 + z, "col": x * 4 + pair * 2 + core}


def turn(v, by):
    return (v + by) % 4


class Post:
    def __init__(self, send_sem, recv_sem):
        self.send_sem = send_sem
        self.recv_sem = recv_sem
        self.sent = []

    def send(self, src, dst, peer):
        at = len(self.sent)
        copy = pltpu.make_async_remote_copy(
            src_ref=src,
            dst_ref=dst,
            send_sem=self.send_sem.at[at],
            recv_sem=self.recv_sem.at[at],
            device_id=peer,
            device_id_type=pl.DeviceIdType.MESH,
        )
        copy.start()
        self.sent.append(copy)
        return copy

    def finish(self):
        for copy in self.sent:
            copy.wait_send()


def count_of(condition):
    return jnp.where(condition, 1, 0).astype(I32)


def iota(shape, axis):
    return lax.broadcasted_iota(I32, shape, axis)


def stand(row):
    eye = iota((EDGE, EDGE), 0) == iota((EDGE, EDGE), 1)
    parts = []
    for t in range(row.shape[1] // EDGE):
        wide = jnp.broadcast_to(row[:, t * EDGE : (t + 1) * EDGE], (EDGE, EDGE))
        parts.append(jnp.sum(jnp.where(eye, wide, jnp.zeros_like(wide)), axis=1, keepdims=True))
    return jnp.concatenate(parts, axis=0)


def order_slots(col_row, row_row, lists, empty):
    slots, spots = col_row.shape[1], lists.shape[1]
    col, row = stand(col_row), stand(row_row)
    earlier = iota((slots, slots), 1) < iota((slots, slots), 0)
    equal = jnp.broadcast_to(col_row, (slots, slots)) == jnp.broadcast_to(col, (slots, slots))
    within = jnp.sum(count_of(equal & earlier), axis=1, keepdims=True)
    hit = jnp.broadcast_to(col, (slots, EDGE)) == iota((slots, EDGE), 1)
    pairs_row = (jnp.sum(count_of(hit), axis=0, keepdims=True) + 1) // 2
    pairs_row = jnp.where(iota((1, EDGE), 1) < TILES, pairs_row, 0)
    pairs_col = stand(pairs_row)
    square = (EDGE, EDGE)
    start_col = jnp.sum(
        jnp.where(iota(square, 1) < iota(square, 0), jnp.broadcast_to(pairs_row, square), 0),
        axis=1, keepdims=True,
    )
    start_row = jnp.sum(
        jnp.where(iota(square, 0) < iota(square, 1), jnp.broadcast_to(pairs_col, square), 0),
        axis=0, keepdims=True,
    )
    start = jnp.sum(
        jnp.where(hit, jnp.broadcast_to(start_row, (slots, EDGE)), 0), axis=1, keepdims=True
    )
    spot = jnp.where(col < TILES, 2 * start + within, -1)
    here = jnp.broadcast_to(spot, (slots, spots)) == iota((slots, spots), 1)
    lists[0:1, :] = empty + jnp.sum(
        jnp.where(here, iota((slots, spots), 0) - empty, 0), axis=0, keepdims=True
    )
    lists[1:2, :] = jnp.sum(
        jnp.where(here, jnp.broadcast_to(row, (slots, spots)), 0), axis=0, keepdims=True
    )
    begins = (jnp.broadcast_to(start_col, (EDGE, spots)) == iota((EDGE, spots), 1)) & (
        jnp.broadcast_to(pairs_col, (EDGE, spots)) > 0
    )
    lists[2:3, :] = 1 - jnp.sum(count_of(begins), axis=0, keepdims=True)
    last = jnp.where(pairs_row > 0, start_row + pairs_row - 1, PAIRS)
    lists[3:4, :] = jnp.concatenate([last, jnp.zeros((1, spots - EDGE), I32)], axis=1)
    lists[4:8, :] = jnp.zeros((4, spots), I32)


def layer_kernel(
    inputs_in, aggregated_in, grad_out_in, preact_in, inv_in, w_self_in, w_neigh_in,
    blocks_in, rows_in, cols_in, count_in, out, weights, bias, *scratch,
):
    (
        inputs, aggregated, grad_out, preact, w_self, w_neigh, masked_ref, self_term,
        blocks, prefix, partial, lists_v, lists,
        shares_y, from_y, shares_z, from_z, shares_x, from_x,
        work_a, from_core, work_b, from_pair, by_z, by_y, by_x,
        inv, block_rows, block_cols, block_count,
        send_sem, recv_sem, load_sem,
    ) = scratch[:33]
    flow_refs = [scratch[33 + i * 7 : 40 + i * 7] for i in range(HALVES * len(FLOWS))]
    strips = scratch[33 + 7 * HALVES * len(FLOWS) :]
    y, z, x, pair, core = place()
    rows, feat = inputs.shape
    cut = feat // HALVES
    right, left, opposite, other = turn(x, 1), turn(x, 3), turn(x, 2), 1 - pair
    to_pair = device(y, z, x, other, core)
    to_core = device(y, z, x, pair, 1 - core)
    peer_y = {by: device(turn(y, by), z, x, pair, core) for by in (1, 2, 3)}
    peer_z = {by: device(y, turn(z, by), x, pair, core) for by in (1, 2, 3)}
    peer_x = {by: device(y, z, turn(x, by), pair, core) for by in (1, 2, 3)}
    to_right, to_left = peer_x[1], peer_x[3]
    met = [to_pair, to_core] + [
        peer[by] for peer in (peer_y, peer_z, peer_x) for by in (1, 2, 3)
    ]
    barrier = pltpu.get_barrier_semaphore()
    for peer in met:
        pl.semaphore_signal(barrier, inc=1, device_id=peer, device_id_type=pl.DeviceIdType.MESH)
    post = Post(send_sem, recv_sem)
    peers = {"y": peer_y, "z": peer_z}
    own = {"y": y, "z": z}

    loads = []

    def load(src, dst):
        copy = pltpu.make_async_copy(src, dst, load_sem.at[len(loads)])
        copy.start()
        loads.append(copy)
        return copy

    half = rows // 2
    first = [load(w_neigh_in, w_neigh), load(inv_in, inv)]
    parts = []
    for h in range(2):
        span = pl.ds(h * half, half)
        parts.append(
            [load(preact_in.at[span], preact.at[span]), load(grad_out_in.at[span], grad_out.at[span])]
        )
    later = [load(w_self_in, w_self), load(inputs_in, inputs), load(aggregated_in, aggregated)]
    slots = blocks_in.shape[0]
    given = [
        load(rows_in, block_rows),
        load(cols_in, block_cols),
        load(count_in, block_count),
    ]
    fetched = load(blocks_in, blocks.at[pl.ds(0, slots)])

    per_shard = rows // EDGE

    def part(at_x, at_pair, at_core, h):
        shard = (at_x * 2 + at_pair) * 2 + at_core
        return pl.ds(shard * per_shard + h * (per_shard // 2), per_shard // 2)

    def gather(f):
        def send(where, peer):
            return post.send(strips[f].at[where], strips[f].at[where], peer)

        passed = []

        def arrived(copy, at_x, at_pair, h):
            copy.wait_recv()
            where = part(at_x, at_pair, core, h)
            passed.append(send(where, to_core))
            return where

        own_right, own_left, own_pair = {}, {}, {}
        for h in range(2):
            mine = part(x, pair, core, h)
            own_right[h] = send(mine, to_right)
            own_left[h] = send(mine, to_left)
            own_pair[h] = send(mine, to_pair)
            passed.append(send(mine, to_core))
            yield
        far_0 = send(arrived(own_right[0], left, pair, 0), to_right)
        arrived(own_left[0], right, pair, 0)
        yield
        where = arrived(own_pair[0], x, other, 0)
        other_right_0, other_left_0 = send(where, to_right), send(where, to_left)
        yield
        far_1 = send(arrived(own_left[1], right, pair, 1), to_left)
        arrived(own_right[1], left, pair, 1)
        yield
        where = arrived(own_pair[1], x, other, 1)
        other_right_1, other_left_1 = send(where, to_right), send(where, to_left)
        yield
        far_pair_0 = send(arrived(far_0, opposite, pair, 0), to_pair)
        far_pair_1 = send(arrived(far_1, opposite, pair, 1), to_pair)
        yield
        arrived(other_right_0, left, other, 0)
        arrived(other_left_0, right, other, 0)
        yield
        arrived(other_right_1, left, other, 1)
        arrived(other_left_1, right, other, 1)
        yield
        arrived(far_pair_0, opposite, other, 0)
        arrived(far_pair_1, opposite, other, 1)
        for copy in passed:
            copy.wait_recv()

    def product(f):
        for begin in range(0, PAIRS, PART):

            def body(u, total):
                for i in range(STRIDE):
                    at = begin + u * STRIDE + i
                    pick = (lists[0, 2 * at], lists[0, 2 * at + 1])
                    line = (lists[1, 2 * at], lists[1, 2 * at + 1])
                    go_on = lists[2, at] == 1
                    total = jnp.where(go_on, total, jnp.zeros_like(total)) + lax.dot_general(
                        jnp.concatenate([blocks[pick[0]], blocks[pick[1]]], axis=0),
                        jnp.concatenate([strips[f][line[0]], strips[f][line[1]]], axis=0),
                        (((0,), (0,)), ((), ())),
                        preferred_element_type=F32,
                    )
                    prefix[at] = total
                return total

            before = prefix[begin - 1] if begin else jnp.zeros((EDGE, cut), F32)
            lax.fori_loop(0, PART // STRIDE, body, before)
            yield

        def leave(g, carry):
            for i in range(4):
                at = g * 4 + i
                span = pl.ds(pl.multiple_of(at * EDGE, EDGE), EDGE)
                partial[f, span, :] = prefix[lists[3, at]].astype(BF16)
            return carry

        lax.fori_loop(0, TILES // 4, leave, 0)

    def flow(refs, f, first, second, offset, span):
        via_a, left_a, right_a, sum_a, hold, via_b, side_b = refs
        h = span // 2
        halves = (slice(0, h), slice(h, span))
        ahead_a, back_a = peers[first][1], peers[first][3]
        ahead_b, back_b = peers[second][1], peers[second][3]
        order = (2, 1, 3, 0)

        def piece(by_a, by_b, k):
            at = {first: turn(own[first], by_a), second: turn(own[second], by_b)}
            start = (at["y"] * 4 + at["z"]) * rows + offset
            if k is None:
                return pl.ds(pl.multiple_of(start, 128), span)
            return pl.ds(pl.multiple_of(start + k * h, 64), h)

        far, near = {}, {}

        def launch(i):
            b = order[i]
            far[i] = (
                post.send(partial.at[f, piece(2, b, 0)], via_a.at[i, 0], ahead_a),
                post.send(partial.at[f, piece(2, b, 1)], via_a.at[i, 1], back_a),
            )
            near[i] = [
                post.send(partial.at[f, piece(1, b, 1)], left_a.at[i, pl.ds(h, h)], ahead_a),
                post.send(partial.at[f, piece(3, b, 0)], right_a.at[i, pl.ds(0, h)], back_a),
            ]

        def relay(i):
            b = order[i]
            far[i][0].wait_recv()
            sum_a[i, 0] = (
                via_a[i, 0].astype(F32) + partial[f, piece(1, b, 0), :].astype(F32)
            ).astype(BF16)
            near[i].append(post.send(sum_a.at[i, 0], left_a.at[i, pl.ds(0, h)], ahead_a))
            far[i][1].wait_recv()
            sum_a[i, 1] = (
                via_a[i, 1].astype(F32) + partial[f, piece(3, b, 1), :].astype(F32)
            ).astype(BF16)
            near[i].append(post.send(sum_a.at[i, 1], right_a.at[i, pl.ds(h, h)], back_a))

        def close(i):
            for copy in near[i]:
                copy.wait_recv()
            return (
                partial[f, piece(0, order[i], None), :].astype(F32)
                + left_a[i].astype(F32)
                + right_a[i].astype(F32)
            )

        launch(0)
        launch(1)
        yield
        sent_b = []
        for i in range(5):
            if i < 4:
                relay(i)
                if i + 2 < 4:
                    launch(i + 2)
                yield
            if i == 0:
                continue
            done = close(i - 1)
            if i == 1:
                hold[0] = done.astype(BF16)
                far_b = (
                    post.send(hold.at[0, pl.ds(0, h)], via_b.at[0], ahead_b),
                    post.send(hold.at[0, pl.ds(h, h)], via_b.at[1], back_b),
                )
            elif i == 2:
                hold[1, pl.ds(h, h), :] = done[halves[1], :].astype(BF16)
                sent_b.append(
                    post.send(hold.at[1, pl.ds(h, h)], side_b.at[0, pl.ds(h, h)], ahead_b)
                )
                far_b[0].wait_recv()
                hold[1, pl.ds(0, h), :] = (done[halves[0], :] + via_b[0].astype(F32)).astype(BF16)
                sent_b.append(
                    post.send(hold.at[1, pl.ds(0, h)], side_b.at[0, pl.ds(0, h)], ahead_b)
                )
            elif i == 3:
                hold[2, pl.ds(0, h), :] = done[halves[0], :].astype(BF16)
                sent_b.append(
                    post.send(hold.at[2, pl.ds(0, h)], side_b.at[1, pl.ds(0, h)], back_b)
                )
                far_b[1].wait_recv()
                hold[2, pl.ds(h, h), :] = (done[halves[1], :] + via_b[1].astype(F32)).astype(BF16)
                sent_b.append(
                    post.send(hold.at[2, pl.ds(h, h)], side_b.at[1, pl.ds(h, h)], back_b)
                )
            else:
                done = done + self_term[pl.ds(offset, span), f * cut : (f + 1) * cut]
                yield
                for copy in sent_b:
                    copy.wait_recv()
                out[pl.ds(offset, span), f * cut : (f + 1) * cut] = (
                    done + side_b[0].astype(F32) + side_b[1].astype(F32)
                ).astype(BF16)
            yield

    def weight_sums():
        copies = [
            post.send(shares_y.at[turn(y, by)], from_y.at[y], peer_y[by]) for by in (1, 2, 3)
        ]
        from_y[y] = shares_y[y]
        yield
        for copy in copies:
            copy.wait_recv()
        total_y = from_y[0] + from_y[1] + from_y[2] + from_y[3]
        for q in range(4):
            shares_z[q, :small, :] = total_y[q * small : (q + 1) * small, :]
            shares_z[q, small:, :] = total_y[tall:, :]
        copies = [
            post.send(shares_z.at[turn(z, by)], from_z.at[z], peer_z[by]) for by in (1, 2, 3)
        ]
        from_z[z] = shares_z[z]
        yield
        for copy in copies:
            copy.wait_recv()
        total_z = from_z[0] + from_z[1] + from_z[2] + from_z[3]
        for q in range(4):
            shares_x[q, :PAD, :] = total_z[q * PAD : (q + 1) * PAD, :]
            shares_x[q, PAD:, :] = total_z[4 * PAD :, :]
        copies = [
            post.send(shares_x.at[turn(x, by)], from_x.at[x], peer_x[by]) for by in (1, 2, 3)
        ]
        from_x[x] = shares_x[x]
        yield
        for copy in copies:
            copy.wait_recv()
        work_a[...] = from_x[0] + from_x[1] + from_x[2] + from_x[3]
        copy = post.send(work_a, from_core, to_core)
        yield
        copy.wait_recv()
        work_b[...] = work_a[...] + from_core[...]
        copy = post.send(work_b, from_pair, to_pair)
        yield
        copy.wait_recv()
        done = work_b[...] + from_pair[...]
        bias[...] = done[PAD:, :]
        by_z[z] = done[:PAD, :]
        copies = [post.send(by_z.at[z], by_z.at[z], peer_z[by]) for by in (1, 2, 3)]
        yield
        for copy in copies:
            copy.wait_recv()
        by_y[y] = by_z[...]
        copies = [post.send(by_z, by_y.at[y], peer_y[by]) for by in (1, 2, 3)]
        yield
        for copy in copies:
            copy.wait_recv()
        by_x[x] = by_y[...]
        copies = [post.send(by_y, by_x.at[x], peer_x[by]) for by in (1, 2, 3)]
        yield
        yield
        for copy in copies:
            copy.wait_recv()
        for at_y in range(4):
            for at_z in range(4):
                for at_x in range(4):
                    first = ((at_y * 4 + at_z) * 4 + at_x) * PAD
                    weights[first : first + PAD, :] = by_x[at_x, at_y, at_z]

    def step(one, count=1):
        for unused in range(count):
            if next(one, "end") == "end":
                return False
        return True

    gathers = [gather(f) for f in range(HALVES)]
    for copy in first:
        copy.wait()
    scales = inv[...].astype(F32).reshape(rows // EDGE, EDGE)
    for h in range(2):
        for copy in parts[h]:
            copy.wait()
        base = h * half
        grads = grad_out[base : base + half, :]
        masked = jnp.where(preact[base : base + half, :] > 0, grads, jnp.zeros_like(grads))
        masked_ref[base : base + half, :] = masked
        projected = lax.dot_general(
            masked, w_neigh[...], (((1,), (1,)), ((), ())), preferred_element_type=F32
        )
        for t in range(half // EDGE):
            at = h * (half // EDGE) + t
            scaled = (projected[t * EDGE : (t + 1) * EDGE, :] * stand(scales[at : at + 1, :])).astype(BF16)
            mine = ((x * 2 + pair) * 2 + core) * per_shard + at
            for f in range(HALVES):
                strips[f][mine] = scaled[:, f * cut : (f + 1) * cut]
        if h == 0:
            pl.semaphore_wait(barrier, len(met))
        step(gathers[0])

    tall = 2 * feat // 4
    small = tall // 4
    for copy in later:
        copy.wait()
    masked = masked_ref[...]
    bias_part = jnp.sum(masked.astype(F32), axis=0, keepdims=True)
    for which, factor in enumerate((inputs, aggregated)):
        result = lax.dot_general(
            factor[...], masked, (((0,), (0,)), ((), ())), preferred_element_type=F32
        )
        for q in range(2):
            shares_y[which * 2 + q, :tall, :] = result[q * tall : (q + 1) * tall, :]
            shares_y[which * 2 + q, tall:, :] = jnp.broadcast_to(bias_part, (PAD, feat))
    sums = weight_sums()
    step(sums)
    step(gathers[0])
    blocks[slots] = jnp.zeros((EDGE, EDGE), BF16)
    prefix[PAIRS] = jnp.zeros((EDGE, cut), F32)
    for copy in given:
        copy.wait()
    spots = slots + -slots % EDGE
    spot = iota((1, spots), 1)

    def line_up(u, rows_of):
        col_row, row_row = rows_of
        for i in range(8):
            at = u * 8 + i
            col_row = jnp.where(spot == at, block_cols[at], col_row)
            row_row = jnp.where(spot == at, block_rows[at], row_row)
        return col_row, row_row

    blank = jnp.zeros((1, spots), I32)
    col_row, row_row = lax.fori_loop(0, slots // 8, line_up, (blank, blank))
    live = spot < block_count[0, 0]
    order_slots(jnp.where(live, col_row, EDGE - 1), row_row, lists_v, slots)
    listed = load(lists_v, lists)
    step(gathers[0])
    self_term[...] = lax.dot_general(
        masked, w_self[...], (((1,), (1,)), ((), ())), preferred_element_type=F32
    )
    listed.wait()
    fetched.wait()
    step(gathers[0], 2)
    for f in range(1, HALVES):
        step(gathers[f], 2)
    while step(gathers[0]):
        pass
    step(sums)

    flows = []
    for f in range(HALVES):
        work = product(f)
        busy = True
        while busy:
            busy = step(work)
            if f + 1 < HALVES:
                step(gathers[f + 1], 2)
            flows = [one for one in flows if step(one)]
            step(sums)
        if f + 1 < HALVES:
            while step(gathers[f + 1]):
                pass
        flows += [
            flow(flow_refs[f * len(FLOWS) + i], f, *spec) for i, spec in enumerate(FLOWS)
        ]
        flows = [one for one in flows if step(one)]
    while flows:
        flows = [one for one in flows if step(one)]
        step(sums)
    while step(sums):
        pass
    post.finish()


def local(
    inputs, aggregated, grad_out, preact, inv_degree, w_self, w_neigh,
    blocks, block_rows, block_cols, block_count,
):
    rows, feat = inputs.shape
    cut = feat // HALVES
    strip_rows = rows * lax.axis_size("col")
    group_rows = rows * lax.axis_size("row")
    vmem = pl.BlockSpec(memory_space=pltpu.VMEM)
    hbm = pl.BlockSpec(memory_space=pltpu.HBM)
    dma = pltpu.SemaphoreType.DMA
    slots = blocks.shape[0]
    tall = 2 * feat // 4
    small = tall // 4
    whole = pltpu.VMEM((rows, feat), BF16)
    square = pltpu.VMEM((feat, feat), BF16)
    two = (2 * PAD, feat)
    sends = HALVES * (30 + 30 * len(FLOWS)) + 20
    scratch = [
        whole, whole, whole, whole, square, square, whole, pltpu.VMEM((rows, feat), F32),
        pltpu.VMEM((slots + 1, EDGE, EDGE), BF16),
        pltpu.VMEM((PAIRS + 1, EDGE, cut), F32),
        pltpu.VMEM((HALVES, group_rows, cut), BF16),
        pltpu.VMEM((8, 512), I32),
        pltpu.SMEM((8, 512), I32),
        pltpu.VMEM((4, tall + PAD, feat), F32),
        pltpu.VMEM((4, tall + PAD, feat), F32),
        pltpu.VMEM((4, small + PAD, feat), F32),
        pltpu.VMEM((4, small + PAD, feat), F32),
        pltpu.VMEM((4,) + two, F32),
        pltpu.VMEM((4,) + two, F32),
        pltpu.VMEM(two, F32),
        pltpu.VMEM(two, F32),
        pltpu.VMEM(two, F32),
        pltpu.VMEM(two, F32),
        pltpu.VMEM((4, PAD, feat), F32),
        pltpu.VMEM((4, 4, PAD, feat), F32),
        pltpu.VMEM((4, 4, 4, PAD, feat), F32),
        pltpu.VMEM((rows,), BF16),
        pltpu.SMEM((slots,), I32),
        pltpu.SMEM((slots,), I32),
        pltpu.SMEM((1, 1), I32),
        dma((sends,)),
        dma((sends,)),
        dma((14,)),
    ]
    for unused in range(HALVES):
        for unused_a, unused_b, unused_c, span in FLOWS:
            scratch += [
                pltpu.VMEM((4, 2, span // 2, cut), BF16),
                pltpu.VMEM((4, span, cut), BF16),
                pltpu.VMEM((4, span, cut), BF16),
                pltpu.VMEM((4, 2, span // 2, cut), BF16),
                pltpu.VMEM((3, span, cut), BF16),
                pltpu.VMEM((2, span // 2, cut), BF16),
                pltpu.VMEM((2, span, cut), BF16),
            ]
    scratch += [pltpu.VMEM((strip_rows // EDGE, EDGE, cut), BF16)] * HALVES
    grad_inputs, weights, bias = pl.pallas_call(
        layer_kernel,
        out_shape=(
            jax.ShapeDtypeStruct((rows, feat), BF16),
            jax.ShapeDtypeStruct((2 * feat, feat), F32),
            jax.ShapeDtypeStruct((PAD, feat), F32),
        ),
        in_specs=[hbm] * 11,
        out_specs=(vmem, vmem, vmem),
        scratch_shapes=scratch,
        compiler_params=pltpu.CompilerParams(
            collective_id=0, has_side_effects=True, vmem_limit_bytes=LIMIT * 2**20
        ),
        name="layer",
    )(
        inputs, aggregated, grad_out, preact, inv_degree, w_self, w_neigh,
        blocks, block_rows, block_cols, block_count,
    )
    return grad_inputs, weights[:feat], weights[feat:], bias[0]


def solution(mesh):
    both = ("row", "col")
    return jax.shard_map(
        local,
        mesh=mesh,
        in_specs=(
            P(both, None), P(both, None), P(both, None), P(both, None), P(both),
            P(), P(),
            P(both, None, None), P(both), P(both), P("row", "col"),
        ),
        out_specs=(P(both, None), P(), P(), P()),
        check_vma=False,
    )
```

time: 428 us -> 96.2 us (0.22)
  matrix products: 203 us -> 0 us
  Pallas kernels: 0 us -> 89.9 us
  blocking collectives: 78.5 us -> 0 us
  other arithmetic: 49.1 us -> 0 us
  local copies, waits for them, and re-layouts: 41.6 us -> 4.78 us
  waiting for transfers between devices: 35.9 us -> 0 us
  between operations: 15.5 us -> 1.29 us
    dot_general x44 -> x0, matrix products: 203 us -> none  [the longest x8 92.7 us: accumulate(): jnp.einsum('kg,kjf->gjf', col_hot, lower_part, preferred_element_type=jnp...]
    pallas_call x0 -> x1, Pallas kernels: none -> 89.9 us  [local(): pl.pallas_call(layer_kernel, out_shape=(jax.ShapeDtypeStruct((rows, feat)...]
    psum x1 -> x0, blocking collectives: 78.5 us -> none  [local(): lax.psum((grad_self, grad_neigh, grad_bias), ('row', 'col'))]
    convert_element_type x18 -> x0, other arithmetic: 37 us -> none  [the longest x8 24.1 us: accumulate(): (remainder - middle_part.astype(jnp.float32)).astype(jnp.bfloat16)]
    all_gather x1 -> x0, waiting for transfers between devices: 23.2 us -> none  [local(): strip_grads = lax.all_gather(local_grads, 'col', axis=0, tiled=True)]
    unnamed x15 -> x1, local copies, waits for them, and re-layouts: 19 us -> 1.67 us
    reduce_scatter x1 -> x0, waiting for transfers between devices: 12.7 us -> none  [local(): lax.psum_scatter(partial_value.reshape(-1, features).astype(jnp.bfloat16)...]
    while x32 -> x0, local copies, waits for them, and re-layouts: 12 us -> none
  transfers between devices with their start and end apart: 3 -> 0, of which waited for: 2 -> 0; matrix products, arithmetic and copies ran while one was open for 65% -> 0% of each run, Pallas kernels for 0% -> 0%
where the time goes in v2:
time: 96.2 us; the launch traced here: 96 us
  Pallas kernels  89.9 us (93%)
  local copies, waits for them, and re-layouts  4.78 us (5%)
  between operations  1.29 us (1%)
    pallas_call x1, Pallas kernels, local(): pl.pallas_call(layer_kernel, out_shape=(jax.ShapeDtypeStruct((rows, feat)...  89.9 us
    slice x2, local copies, waits for them, and re-layouts, local(): return (grad_inputs, weights[:feat], weights[feat:], bias[0])  3.11 us

profile of v2, /device:TPU:32, one launch (start us, length us, event | category | flops | bytes accessed | tf_op | source)
XLA Modules:
  0.0 96.0 jit_solution(15781431424030352896)
XLA Ops:
  1.3 89.9 %layer.1 = (bf16[512,256]{1,0:T(8,128)(2,1)}, f32[512,256]{1,0:T(8,128)}, f32[8,256]{1,0:T(8,128)}) custom-call(bf16[512,256]{1,0:T(8,128)(2,1)} %inputs_in.1, bf16[512,256]{1,0:T(8,128)(2,1)} %aggregated_in.1, bf16[512,256]{1,0:T(8,128)(2,1)} %grad_out_in.1, bf16[512,256]{1,0:T(8,128)(2,1)} %preact_in.1, bf16[512]{0:T(512)(128)(2,1)} %inv_in.1, ...), custom_call_target="tpu_custom_call" | custom-call | tf_op jit(solution)/shard_map/layer/pallas_call | solution.py:584
  91.2 1.3 %slice.11 = f32[1,256]{1,0:T(1,128)} slice(f32[8,256]{1,0:T(8,128)} %get-tuple-element.9), slice={[0:1], [0:256]} | slice | bytes 2048 | tf_op jit(solution)/shard_map/slice | solution.py:602
  92.5 1.9 %fusion = (f32[256,256]{1,0:T(8,128)}, f32[256,256]{1,0:T(8,128)}) fusion(f32[512,256]{1,0:T(8,128)} %get-tuple-element.8), kind=kLoop, calls=%fused_computation | loop fusion | bytes 1048576 | tf_op jit(solution)/shard_map/slice | solution.py:602
  94.3 1.7 %copy.17 = bf16[512,256]{1,0:T(8,128)(2,1)} copy(bf16[512,256]{1,0:T(8,128)(2,1)} %get-tuple-element.16) | data formatting | bytes 524288

commit v3 on v2

--- a/solution.py
+++ b/solution.py
@@ -16,6 +16,7 @@
 FLOWS = (("y", "z", 0, 384), ("z", "y", 384, 128))
 PAD = 8
 LIMIT = 62
+SUM_TURNS = (3, 6, 8, 10, 12, 15, 18, 21)
 PAIRS = 200
 STRIDE = 20
 PART = 40
@@ -118,18 +119,18 @@
 
 def layer_kernel(
     inputs_in, aggregated_in, grad_out_in, preact_in, inv_in, w_self_in, w_neigh_in,
-    blocks_in, rows_in, cols_in, count_in, out, weights, bias, *scratch,
+    blocks_in, rows_in, cols_in, count_in, out_hbm, weights_hbm, bias_hbm, *scratch,
 ):
     (
         inputs, aggregated, grad_out, preact, w_self, w_neigh, masked_ref, self_term,
         blocks, prefix, partial, lists_v, lists,
         shares_y, from_y, shares_z, from_z, shares_x, from_x,
         work_a, from_core, work_b, from_pair, by_z, by_y, by_x,
-        inv, block_rows, block_cols, block_count,
+        inv, block_rows, block_cols, block_count, out, weights, bias,
         send_sem, recv_sem, load_sem,
-    ) = scratch[:33]
-    flow_refs = [scratch[33 + i * 7 : 40 + i * 7] for i in range(HALVES * len(FLOWS))]
-    strips = scratch[33 + 7 * HALVES * len(FLOWS) :]
+    ) = scratch[:36]
+    flow_refs = [scratch[36 + i * 7 : 43 + i * 7] for i in range(HALVES * len(FLOWS))]
+    strips = scratch[36 + 7 * HALVES * len(FLOWS) :]
     y, z, x, pair, core = place()
     rows, feat = inputs.shape
     cut = feat // HALVES
@@ -410,7 +411,6 @@
         by_x[x] = by_y[...]
         copies = [post.send(by_y, by_x.at[x], peer_x[by]) for by in (1, 2, 3)]
         yield
-        yield
         for copy in copies:
             copy.wait_recv()
         for at_y in range(4):
@@ -448,66 +448,84 @@
         if h == 0:
             pl.semaphore_wait(barrier, len(met))
         step(gathers[0])
+    for f in range(1, HALVES):
+        step(gathers[f], 2)
 
     tall = 2 * feat // 4
     small = tall // 4
-    for copy in later:
-        copy.wait()
-    masked = masked_ref[...]
-    bias_part = jnp.sum(masked.astype(F32), axis=0, keepdims=True)
-    for which, factor in enumerate((inputs, aggregated)):
+
+    def sort_chore():
+        blocks[slots] = jnp.zeros((EDGE, EDGE), BF16)
+        prefix[PAIRS] = jnp.zeros((EDGE, cut), F32)
+        for copy in given:
+            copy.wait()
+        spots = slots + -slots % EDGE
+        spot = iota((1, spots), 1)
+
+        def line_up(u, rows_of):
+            col_row, row_row = rows_of
+            for i in range(8):
+                at = u * 8 + i
+                col_row = jnp.where(spot == at, block_cols[at], col_row)
+                row_row = jnp.where(spot == at, block_rows[at], row_row)
+            return col_row, row_row
+
+        blank = jnp.zeros((1, spots), I32)
+        col_row, row_row = lax.fori_loop(0, slots // 8, line_up, (blank, blank))
+        live = spot < block_count[0, 0]
+        order_slots(jnp.where(live, col_row, EDGE - 1), row_row, lists_v, slots)
+        return load(lists_v, lists)
+
+    def weight_chore(which, factor):
         result = lax.dot_general(
-            factor[...], masked, (((0,), (0,)), ((), ())), preferred_element_type=F32
+            factor[...], masked_ref[...], (((0,), (0,)), ((), ())), preferred_element_type=F32
         )
         for q in range(2):
             shares_y[which * 2 + q, :tall, :] = result[q * tall : (q + 1) * tall, :]
-            shares_y[which * 2 + q, tall:, :] = jnp.broadcast_to(bias_part, (PAD, feat))
+
+    def bias_chore():
+        bias_part = jnp.sum(masked_ref[...].astype(F32), axis=0, keepdims=True)
+        for q in range(4):
+            shares_y[q, tall:, :] = jnp.broadcast_to(bias_part, (PAD, feat))
+
     sums = weight_sums()
+    listed = sort_chore()
+    step(gathers[0], 2)
+    later[0].wait()
+    self_term[...] = lax.dot_general(
+        masked_ref[...], w_self[...], (((1,), (1,)), ((), ())), preferred_element_type=F32
+    )
+    step(gathers[0], 2)
+    later[1].wait()
+    weight_chore(0, inputs)
+    step(gathers[0])
+    step(gathers[1])
+    later[2].wait()
+    weight_chore(1, aggregated)
+    step(gathers[1])
+    bias_chore()
     step(sums)
     step(gathers[0])
-    blocks[slots] = jnp.zeros((EDGE, EDGE), BF16)
-    prefix[PAIRS] = jnp.zeros((EDGE, cut), F32)
-    for copy in given:
-        copy.wait()
-    spots = slots + -slots % EDGE
-    spot = iota((1, spots), 1)
-
-    def line_up(u, rows_of):
-        col_row, row_row = rows_of
-        for i in range(8):
-            at = u * 8 + i
-            col_row = jnp.where(spot == at, block_cols[at], col_row)
-            row_row = jnp.where(spot == at, block_rows[at], row_row)
-        return col_row, row_row
-
-    blank = jnp.zeros((1, spots), I32)
-    col_row, row_row = lax.fori_loop(0, slots // 8, line_up, (blank, blank))
-    live = spot < block_count[0, 0]
-    order_slots(jnp.where(live, col_row, EDGE - 1), row_row, lists_v, slots)
-    listed = load(lists_v, lists)
+    step(gathers[1])
     step(gathers[0])
-    self_term[...] = lax.dot_general(
-        masked, w_self[...], (((1,), (1,)), ((), ())), preferred_element_type=F32
-    )
+    step(gathers[1])
+    step(gathers[0])
     listed.wait()
     fetched.wait()
-    step(gathers[0], 2)
-    for f in range(1, HALVES):
-        step(gathers[f], 2)
-    while step(gathers[0]):
-        pass
-    step(sums)
 
     flows = []
+    turns = 0
     for f in range(HALVES):
         work = product(f)
         busy = True
         while busy:
             busy = step(work)
             if f + 1 < HALVES:
-                step(gathers[f + 1], 2)
+                step(gathers[f + 1])
             flows = [one for one in flows if step(one)]
-            step(sums)
+            turns += 1
+            if turns in SUM_TURNS:
+                step(sums)
         if f + 1 < HALVES:
             while step(gathers[f + 1]):
                 pass
@@ -517,10 +535,39 @@
         flows = [one for one in flows if step(one)]
     while flows:
         flows = [one for one in flows if step(one)]
-        step(sums)
+        turns += 1
+        if turns in SUM_TURNS:
+            step(sums)
     while step(sums):
         pass
+    results = [
+        load(out, out_hbm), load(weights, weights_hbm), load(bias, bias_hbm)
+    ]
     post.finish()
+    for copy in results:
+        copy.wait()
+
+
+def leave_kernel(
+    grads, weights, bias, grads_out, self_out, neigh_out, bias_out,
+    grads_v, self_v, neigh_v, bias_v, sem_in, sem_out,
+):
+    feat = weights.shape[1]
+    moves = (
+        (weights.at[pl.ds(0, feat)], self_v, self_v, self_out),
+        (weights.at[pl.ds(feat, feat)], neigh_v, neigh_v, neigh_out),
+        (grads, grads_v, grads_v, grads_out),
+        (bias, bias_v, bias_v.at[pl.ds(0, 1)], bias_out),
+    )
+    come = [pltpu.make_async_copy(m[0], m[1], sem_in.at[i]) for i, m in enumerate(moves)]
+    go = [pltpu.make_async_copy(m[2], m[3], sem_out.at[i]) for i, m in enumerate(moves)]
+    for copy in come:
+        copy.start()
+    for arrival, departure in zip(come, go):
+        arrival.wait()
+        departure.start()
+    for copy in go:
+        copy.wait()
 
 
 def local(
@@ -531,7 +578,6 @@
     cut = feat // HALVES
     strip_rows = rows * lax.axis_size("col")
     group_rows = rows * lax.axis_size("row")
-    vmem = pl.BlockSpec(memory_space=pltpu.VMEM)
     hbm = pl.BlockSpec(memory_space=pltpu.HBM)
     dma = pltpu.SemaphoreType.DMA
     slots = blocks.shape[0]
@@ -565,9 +611,12 @@
         pltpu.SMEM((slots,), I32),
         pltpu.SMEM((slots,), I32),
         pltpu.SMEM((1, 1), I32),
+        whole,
+        pltpu.VMEM((2 * feat, feat), F32),
+        pltpu.VMEM((PAD, feat), F32),
         dma((sends,)),
         dma((sends,)),
-        dma((14,)),
+        dma((20,)),
     ]
     for unused in range(HALVES):
         for unused_a, unused_b, unused_c, span in FLOWS:
@@ -581,7 +630,7 @@
                 pltpu.VMEM((2, span, cut), BF16),
             ]
     scratch += [pltpu.VMEM((strip_rows // EDGE, EDGE, cut), BF16)] * HALVES
-    grad_inputs, weights, bias = pl.pallas_call(
+    results = pl.pallas_call(
         layer_kernel,
         out_shape=(
             jax.ShapeDtypeStruct((rows, feat), BF16),
@@ -589,7 +638,7 @@
             jax.ShapeDtypeStruct((PAD, feat), F32),
         ),
         in_specs=[hbm] * 11,
-        out_specs=(vmem, vmem, vmem),
+        out_specs=(hbm, hbm, hbm),
         scratch_shapes=scratch,
         compiler_params=pltpu.CompilerParams(
             collective_id=0, has_side_effects=True, vmem_limit_bytes=LIMIT * 2**20
@@ -599,7 +648,24 @@
         inputs, aggregated, grad_out, preact, inv_degree, w_self, w_neigh,
         blocks, block_rows, block_cols, block_count,
     )
-    return grad_inputs, weights[:feat], weights[feat:], bias[0]
+    square_out = pltpu.VMEM((feat, feat), F32)
+    grad_inputs, grad_self, grad_neigh, grad_bias = pl.pallas_call(
+        leave_kernel,
+        out_shape=(
+            jax.ShapeDtypeStruct((rows, feat), BF16),
+            jax.ShapeDtypeStruct((feat, feat), F32),
+            jax.ShapeDtypeStruct((feat, feat), F32),
+            jax.ShapeDtypeStruct((1, feat), F32),
+        ),
+        in_specs=[hbm] * 3,
+        out_specs=[hbm] * 4,
+        scratch_shapes=[
+            whole, square_out, square_out, pltpu.VMEM((PAD, feat), F32), dma((4,)), dma((4,)),
+        ],
+        compiler_params=pltpu.CompilerParams(vmem_limit_bytes=LIMIT * 2**20),
+        name="leave",
+    )(*results)
+    return grad_inputs, grad_self, grad_neigh, grad_bias.reshape(feat)
 
 
 def solution(mesh):

time: 96.2 us -> 81.9 us (0.85); the launches traced: 96 us -> 80.3 us
  Pallas kernels: 89.9 us -> 79 us
  local copies, waits for them, and re-layouts: 4.78 us -> 0 us
    pallas_call x1, Pallas kernels: 89.9 us -> 77.1 us  [local(): pl.pallas_call(layer_kernel, out_shape=(jax.ShapeDtypeStruct((rows, feat)...]
    slice x2 -> x0, local copies, waits for them, and re-layouts: 3.11 us -> none  [local(): return (grad_inputs, weights[:feat], weights[feat:], bias[0])]
    pallas_call x0 -> x1, Pallas kernels: none -> 1.9 us  [local(): pl.pallas_call(leave_kernel, out_shape=(jax.ShapeDtypeStruct((rows, feat)...]
    unnamed x1 -> x0, local copies, waits for them, and re-layouts: 1.67 us -> none
where the time goes in v3:
time: 81.9 us; the launch traced here: 80.3 us
  Pallas kernels  79 us (96%)
  between operations  1.29 us (2%)
    pallas_call x1, Pallas kernels, local(): pl.pallas_call(layer_kernel, out_shape=(jax.ShapeDtypeStruct((rows, feat)...  77.1 us
    pallas_call x1, Pallas kernels, local(): pl.pallas_call(leave_kernel, out_shape=(jax.ShapeDtypeStruct((rows, feat)...  1.9 us

profile of v3, /device:TPU:32, one launch (start us, length us, event | category | flops | bytes accessed | tf_op | source)
XLA Modules:
  0.0 80.3 jit_solution(17514750967897185032)
XLA Ops:
  1.3 77.1 %layer.1 = (bf16[512,256]{1,0:T(8,128)(2,1)}, f32[512,256]{1,0:T(8,128)}, f32[8,256]{1,0:T(8,128)}) custom-call(bf16[512,256]{1,0:T(8,128)(2,1)} %inputs_in.1, bf16[512,256]{1,0:T(8,128)(2,1)} %aggregated_in.1, bf16[512,256]{1,0:T(8,128)(2,1)} %grad_out_in.1, bf16[512,256]{1,0:T(8,128)(2,1)} %preact_in.1, bf16[512]{0:T(512)(128)(2,1)} %inv_in.1, ...), custom_call_target="tpu_custom_call" | custom-call | tf_op jit(solution)/shard_map/layer/pallas_call | solution.py:633
  78.4 1.9 %leave.1 = (bf16[512,256]{1,0:T(8,128)(2,1)}, f32[256,256]{1,0:T(8,128)}, f32[256,256]{1,0:T(8,128)}, f32[1,256]{1,0:T(1,128)}) custom-call(bf16[512,256]{1,0:T(8,128)(2,1)} %get-tuple-element.11.grads, f32[512,256]{1,0:T(8,128)} %get-tuple-element.12.weights, f32[8,256]{1,0:T(8,128)} %get-tuple-element.13.bias), custom_call_target="tpu_custom_call" | custom-call | tf_op jit(solution)/shard_map/leave/pallas_call | solution.py:652

commit v4 on v3

--- a/solution.py
+++ b/solution.py
@@ -366,10 +366,10 @@
         yield
         for copy in copies:
             copy.wait_recv()
-        total_y = from_y[0] + from_y[1] + from_y[2] + from_y[3]
+        total_y = sum(from_y[i].astype(F32) for i in range(4))
         for q in range(4):
-            shares_z[q, :small, :] = total_y[q * small : (q + 1) * small, :]
-            shares_z[q, small:, :] = total_y[tall:, :]
+            shares_z[q, :small, :] = total_y[q * small : (q + 1) * small, :].astype(BF16)
+            shares_z[q, small:, :] = total_y[tall:, :].astype(BF16)
         copies = [
             post.send(shares_z.at[turn(z, by)], from_z.at[z], peer_z[by]) for by in (1, 2, 3)
         ]
@@ -377,10 +377,10 @@
         yield
         for copy in copies:
             copy.wait_recv()
-        total_z = from_z[0] + from_z[1] + from_z[2] + from_z[3]
+        total_z = sum(from_z[i].astype(F32) for i in range(4))
         for q in range(4):
             shares_x[q, :PAD, :] = total_z[q * PAD : (q + 1) * PAD, :]
-            shares_x[q, PAD:, :] = total_z[4 * PAD :, :]
+            shares_x[q, PAD:, :] = total_z[4 * PAD : 5 * PAD, :]
         copies = [
             post.send(shares_x.at[turn(x, by)], from_x.at[x], peer_x[by]) for by in (1, 2, 3)
         ]
@@ -481,12 +481,12 @@
             factor[...], masked_ref[...], (((0,), (0,)), ((), ())), preferred_element_type=F32
         )
         for q in range(2):
-            shares_y[which * 2 + q, :tall, :] = result[q * tall : (q + 1) * tall, :]
+            shares_y[which * 2 + q, :tall, :] = result[q * tall : (q + 1) * tall, :].astype(BF16)
 
     def bias_chore():
         bias_part = jnp.sum(masked_ref[...].astype(F32), axis=0, keepdims=True)
         for q in range(4):
-            shares_y[q, tall:, :] = jnp.broadcast_to(bias_part, (PAD, feat))
+            shares_y[q, tall:, :] = jnp.broadcast_to(bias_part, (2 * PAD, feat)).astype(BF16)
 
     sums = weight_sums()
     listed = sort_chore()
@@ -594,10 +594,10 @@
         pltpu.VMEM((HALVES, group_rows, cut), BF16),
         pltpu.VMEM((8, 512), I32),
         pltpu.SMEM((8, 512), I32),
-        pltpu.VMEM((4, tall + PAD, feat), F32),
-        pltpu.VMEM((4, tall + PAD, feat), F32),
-        pltpu.VMEM((4, small + PAD, feat), F32),
-        pltpu.VMEM((4, small + PAD, feat), F32),
+        pltpu.VMEM((4, tall + 2 * PAD, feat), BF16),
+        pltpu.VMEM((4, tall + 2 * PAD, feat), BF16),
+        pltpu.VMEM((4, small + 2 * PAD, feat), BF16),
+        pltpu.VMEM((4, small + 2 * PAD, feat), BF16),
         pltpu.VMEM((4,) + two, F32),
         pltpu.VMEM((4,) + two, F32),
         pltpu.VMEM(two, F32),

time: 81.9 us -> 80.2 us (0.979)
  Pallas kernels: 79 us -> 77.7 us
    pallas_call x1, Pallas kernels: 77.1 us -> 75.8 us  [local(): pl.pallas_call(layer_kernel, out_shape=(jax.ShapeDtypeStruct((rows, feat)...]
where the time goes in v4:
time: 80.2 us; the launch traced here: 79 us
  Pallas kernels  77.7 us (97%)
  between operations  1.29 us (2%)
    pallas_call x1, Pallas kernels, local(): pl.pallas_call(layer_kernel, out_shape=(jax.ShapeDtypeStruct((rows, feat)...  75.8 us
    pallas_call x1, Pallas kernels, local(): pl.pallas_call(leave_kernel, out_shape=(jax.ShapeDtypeStruct((rows, feat)...  1.9 us

profile of v4, /device:TPU:32, one launch (start us, length us, event | category | flops | bytes accessed | tf_op | source)
XLA Modules:
  0.0 79.0 jit_solution(15436237380504229154)
XLA Ops:
  1.3 75.8 %layer.1 = (bf16[512,256]{1,0:T(8,128)(2,1)}, f32[512,256]{1,0:T(8,128)}, f32[8,256]{1,0:T(8,128)}) custom-call(bf16[512,256]{1,0:T(8,128)(2,1)} %inputs_in.1, bf16[512,256]{1,0:T(8,128)(2,1)} %aggregated_in.1, bf16[512,256]{1,0:T(8,128)(2,1)} %grad_out_in.1, bf16[512,256]{1,0:T(8,128)(2,1)} %preact_in.1, bf16[512]{0:T(512)(128)(2,1)} %inv_in.1, ...), custom_call_target="tpu_custom_call" | custom-call | tf_op jit(solution)/shard_map/layer/pallas_call | solution.py:633
  77.1 1.9 %leave.1 = (bf16[512,256]{1,0:T(8,128)(2,1)}, f32[256,256]{1,0:T(8,128)}, f32[256,256]{1,0:T(8,128)}, f32[1,256]{1,0:T(1,128)}) custom-call(bf16[512,256]{1,0:T(8,128)(2,1)} %get-tuple-element.11.grads, f32[512,256]{1,0:T(8,128)} %get-tuple-element.12.weights, f32[8,256]{1,0:T(8,128)} %get-tuple-element.13.bias), custom_call_target="tpu_custom_call" | custom-call | tf_op jit(solution)/shard_map/leave/pallas_call | solution.py:652

commit v5 on v4

--- a/solution.py
+++ b/solution.py
@@ -522,7 +522,8 @@
             busy = step(work)
             if f + 1 < HALVES:
                 step(gathers[f + 1])
-            flows = [one for one in flows if step(one)]
+            if turns % 2:
+                flows = [one for one in flows if step(one)]
             turns += 1
             if turns in SUM_TURNS:
                 step(sums)

time: 80.2 us -> 79.2 us (0.988)
  Pallas kernels: 77.7 us -> 76.6 us
    pallas_call x1, Pallas kernels: 75.8 us -> 74.7 us  [local(): pl.pallas_call(layer_kernel, out_shape=(jax.ShapeDtypeStruct((rows, feat)...]
where the time goes in v5:
time: 79.2 us; the launch traced here: 77.9 us
  Pallas kernels  76.6 us (97%)
  between operations  1.29 us (2%)
    pallas_call x1, Pallas kernels, local(): pl.pallas_call(layer_kernel, out_shape=(jax.ShapeDtypeStruct((rows, feat)...  74.7 us
    pallas_call x1, Pallas kernels, local(): pl.pallas_call(leave_kernel, out_shape=(jax.ShapeDtypeStruct((rows, feat)...  1.9 us

profile of v5, /device:TPU:32, one launch (start us, length us, event | category | flops | bytes accessed | tf_op | source)
XLA Modules:
  0.0 77.9 jit_solution(15393419716955558452)
XLA Ops:
  1.3 74.7 %layer.1 = (bf16[512,256]{1,0:T(8,128)(2,1)}, f32[512,256]{1,0:T(8,128)}, f32[8,256]{1,0:T(8,128)}) custom-call(bf16[512,256]{1,0:T(8,128)(2,1)} %inputs_in.1, bf16[512,256]{1,0:T(8,128)(2,1)} %aggregated_in.1, bf16[512,256]{1,0:T(8,128)(2,1)} %grad_out_in.1, bf16[512,256]{1,0:T(8,128)(2,1)} %preact_in.1, bf16[512]{0:T(512)(128)(2,1)} %inv_in.1, ...), custom_call_target="tpu_custom_call" | custom-call | tf_op jit(solution)/shard_map/layer/pallas_call | solution.py:634
  76.0 1.9 %leave.1 = (bf16[512,256]{1,0:T(8,128)(2,1)}, f32[256,256]{1,0:T(8,128)}, f32[256,256]{1,0:T(8,128)}, f32[1,256]{1,0:T(1,128)}) custom-call(bf16[512,256]{1,0:T(8,128)(2,1)} %get-tuple-element.11.grads, f32[512,256]{1,0:T(8,128)} %get-tuple-element.12.weights, f32[8,256]{1,0:T(8,128)} %get-tuple-element.13.bias), custom_call_target="tpu_custom_call" | custom-call | tf_op jit(solution)/shard_map/leave/pallas_call | solution.py:653
